TPU v7x, 32 devices: a whole 2x2x4 slice. The times are simulated.
32 devices in a mesh: seq: 16 (over z, y, x), ch: 2 (over core).
Axes of the slice: x: 2, y: 2, z: 4, core: 2. Of those that a mesh axis runs over, the one named last changes fastest.
Arguments:
- q_proj: bfloat16 [2048, 4096], P('seq', 'ch'), may hold values from -16 to 16
- k_proj: bfloat16 [2048, 4096], P('seq', 'ch'), may hold values from -6 to 6
- v_proj: bfloat16 [2048, 4096], P('seq', 'ch'), may hold values from -6 to 6
- feat_filter: float32 [3, 3, 4096], P(None, None, 'ch'), may hold values from -3.5 to 3.5
- long_filter: float32 [2048, 4096], P('seq', 'ch'), may hold values from -0.125 to 0.125
- skip_bias: float32 [4096], P('ch'), may hold values from -4 to 4
- norm_gain: float32 [4096], P('ch'), may hold values from 0.1 to 1.9
Outputs:
- mixed_out: bfloat16 [2048, 4096], P('seq', 'ch')
- normed: bfloat16 [2048, 4096], P('seq', 'ch')
All inputs are finite; a program needn't handle non-finite values.
Results may differ from a plain program's by a relative error of at most 0.015.
Values may be sent and summed in bfloat16 or wider, within the bound.
A program may use at most 64 MiB of HBM per device.

v0:
```python
import math

import jax
import jax.numpy as jnp
from jax import lax
from jax.sharding import PartitionSpec as P

D = 4096


highest_precision = lax.Precision.HIGHEST


def shifted(block, axis, distance):
    devices = range(lax.axis_size(axis))
    route = [(i - distance, i) for i in devices if i - distance in devices]
    return lax.ppermute(block, axis, route)


def for_sending(value):
    return jax.tree.map(lambda a: a.astype(jnp.bfloat16) if a.dtype == jnp.float32 else a, value)


def angle_table(count, left, right):
    product = left[:, None] * right[None, :] % count
    angle = product.astype(jnp.float32) * (2.0 * math.pi / count)
    return (jnp.cos(angle), jnp.sin(angle))


def contract(pattern, table, values):
    return jnp.einsum(pattern, table, values, precision=highest_precision)


def rotate(pattern, cos_table, sin_table, real_part, imag_part, turning):
    out_real = contract(pattern, cos_table, real_part) - turning * contract(
        pattern, sin_table, imag_part
    )
    out_imag = contract(pattern, cos_table, imag_part) + turning * contract(
        pattern, sin_table, real_part
    )
    return (out_real, out_imag)


def frequency_order(groups):
    return jnp.arange(2 * groups, dtype=jnp.int32)


def shards(q_proj, k_proj, v_proj, feat_filter, long_filter, skip_bias, norm_gain):
    rows = q_proj.shape[0]
    taps = feat_filter.shape[1]
    groups = lax.axis_size("seq")
    stacked = jnp.stack([q_proj, k_proj, v_proj])
    previous = shifted(stacked[:, rows - (taps - 1) :, :], "seq", 1)
    extended = jnp.concatenate([previous, stacked], axis=1)
    featured = jnp.zeros(stacked.shape, jnp.float32)
    for offset in range(taps):
        window = extended[:, taps - 1 - offset : taps - 1 - offset + rows, :]
        featured = featured + feat_filter[:, offset, None, :] * window.astype(jnp.float32)
    query = featured[0]
    gated = featured[1] * featured[2]
    device = lax.axis_index("seq")
    per_device = rows // groups
    length = 2 * rows * groups
    order = frequency_order(groups)
    blocks = jnp.arange(groups, dtype=jnp.int32)
    within = jnp.arange(rows, dtype=jnp.int32)
    local_rows = device * per_device + jnp.arange(per_device, dtype=jnp.int32)
    slots = lax.dynamic_slice_in_dim(order, 2 * device, 2)
    cos_a, sin_a = angle_table(2 * groups, order, blocks)
    cos_w, sin_w = angle_table(length, order, local_rows)
    cos_b, sin_b = angle_table(rows, within, within)
    cos_v, sin_v = angle_table(length, slots, within)
    cos_i, sin_i = angle_table(2 * groups, blocks, order)
    signals = jnp.stack([gated, long_filter])[:, None]
    pieces = lax.all_to_all(
        signals.astype(jnp.bfloat16), "seq", split_axis=2, concat_axis=1, tiled=True
    ).astype(signals.dtype)
    real_part = contract("ka,xabc->xkbc", cos_a, pieces)
    imag_part = -contract("ka,xabc->xkbc", sin_a, pieces)
    cosine = cos_w[:, :, None]
    sine = sin_w[:, :, None]
    real_part, imag_part = (
        real_part * cosine + imag_part * sine,
        imag_part * cosine - real_part * sine,
    )
    spread = jnp.stack([real_part, imag_part], axis=1)
    pieces = lax.all_to_all(
        for_sending(spread), "seq", split_axis=2, concat_axis=3, tiled=True
    ).astype(spread.dtype)
    real_part, imag_part = rotate("kb,xsbc->xskc", cos_b, sin_b, pieces[:, 0], pieces[:, 1], -1.0)
    prod_real = real_part[0] * real_part[1] - imag_part[0] * imag_part[1]
    prod_imag = real_part[0] * imag_part[1] + imag_part[0] * real_part[1]
    real_part = prod_real
    imag_part = prod_imag
    real_part, imag_part = rotate("bk,skc->sbc", cos_b, sin_b, real_part, imag_part, 1.0)
    cosine = cos_v[:, :, None]
    sine = sin_v[:, :, None]
    spectra = jnp.stack(
        [real_part * cosine - imag_part * sine, imag_part * cosine + real_part * sine]
    )
    pieces = lax.all_to_all(
        for_sending(spectra), "seq", split_axis=2, concat_axis=1, tiled=True
    ).astype(spectra.dtype)
    summed = contract("ak,kbc->abc", cos_i, pieces[0]) - contract("ak,kbc->abc", sin_i, pieces[1])
    returned = summed / length
    long_conv = lax.all_to_all(
        for_sending(returned), "seq", split_axis=0, concat_axis=1, tiled=True
    ).astype(returned.dtype)[0]
    mixed = query * (long_conv + skip_bias * gated)
    squares = lax.psum(jnp.sum(mixed * mixed, axis=1), "ch")
    scale = lax.rsqrt(squares / D + 1e-05)
    normed = (mixed * scale[:, None] * norm_gain).astype(jnp.bfloat16)
    return (mixed.astype(jnp.bfloat16), normed)


def solution(mesh):
    return jax.shard_map(
        shards,
        mesh=mesh,
        in_specs=(
            P("seq", "ch"),
            P("seq", "ch"),
            P("seq", "ch"),
            P(None, None, "ch"),
            P("seq", "ch"),
            P("ch"),
            P("ch"),
        ),
        out_specs=(P("seq", "ch"), P("seq", "ch")),
        check_vma=False,
    )
```

profile of v0, /device:TPU:0, one launch (start us, length us, event | category | flops | bytes accessed | tf_op | source)
XLA Modules:
  0.0 278.7 jit_solution(3232502488996589101)
XLA Ops:
  0.7 1.7 pad_maximum_fusion.2
  2.4 4.8 %collective-permute-start = (bf16[3,2,2048]{2,1,0:T(2,128)(2,1)S(1)}, bf16[3,2,2048]{2,1,0:T(2,128)(2,1)S(1)}, u32[]{:S(2)}, u32[]{:S(2)}) collective-permute-start(bf16[3,2,2048]{2,1,0:T(2,128)(2,1)S(1)} %slice.74), channel_id=1, source_target_pairs={{0,2},{2,4},{4,6},{6,8},{8,10},{10,12},{12,14},{14,16},{16,18},{18... | collective-permute-start | bytes 73736 | tf_op jit(solution)/shard_map/ppermute | solution.py:17
  10.4 2.1 copy.33
  12.5 8.3 %all-to-all-start = ((bf16[2,1,128,2048]{3,0,1,2:T(2,128)(2,1)}), bf16[2,1,128,2048]{3,0,1,2:T(2,128)(2,1)}, u32[]{:S(2)}, u32[]{:S(2)}) async-start(bf16[2,1,128,2048]{3,0,1,2:T(2,128)(2,1)} %copy.33), calls=%async_computation | async-start | bytes 2097152 | tf_op jit(solution)/shard_map/all_to_all | solution.py:75
  20.9 23.2 %all-to-all-done = bf16[2,1,128,2048]{3,0,1,2:T(2,128)(2,1)} async-done(((bf16[2,1,128,2048]{3,0,1,2:T(2,128)(2,1)}), bf16[2,1,128,2048]{3,0,1,2:T(2,128)(2,1)}, u32[]{:S(2)}, u32[]{:S(2)}) %all-to-all-start) | async-done | bytes 1048608 | tf_op jit(solution)/shard_map/all_to_all | solution.py:75
  44.1 1.6 copy.71
  45.7 2.6 fusion.19
  48.3 3.1 %fusion.7 = (bf16[2,1,32,8,2048]{4,2,3,0,1:T(8,128)(2,1)S(1)}, bf16[2,1,32,8,2048]{4,2,3,0,1:T(8,128)(2,1)S(1)}) fusion(f32[2,8,2048,32]{2,3,1,0:T(8,128)S(1)} %fusion.19, f32[32,8]{0,1:T(8,128)S(1)} %get-tuple-element.20, f32[32,8]{0,1:T(8,128)S(1)} %get-tuple-element.19, bf16[2,16,8,2048]{3,2,1,0:T(8,128)(2,1)S(1)} %bitcast.163), kind=kOutput, calls=%fused_computation.19 | convolution fusion | flops 210770944 | bytes 9439232 | tf_op jit(solution)/shard_map/ka,xabc->xkbc/dot_general | solution.py:31
  51.8 4.3 %copy.37 = bf16[2,2,32,8,2048]{4,3,0,1,2:T(8,128)(2,1)} copy(bf16[2,2,32,8,2048]{4,2,3,0,1:T(8,128)(2,1)S(1)} %pad_maximum_fusion) | data formatting | bytes 8388608 | tf_op jit(solution)/shard_map/stack | solution.py:86
  56.0 6.1 %all-to-all-start.1 = ((bf16[2,2,32,8,2048]{4,3,0,1,2:T(8,128)(2,1)}), bf16[2,2,32,8,2048]{4,3,0,1,2:T(8,128)(2,1)}, u32[]{:S(2)}, u32[]{:S(2)}) async-start(bf16[2,2,32,8,2048]{4,3,0,1,2:T(8,128)(2,1)} %copy.37), calls=%async_computation.1 | async-start | bytes 8388608 | tf_op jit(solution)/shard_map/all_to_all | solution.py:87
  62.3 77.5 %all-to-all-done.1 = bf16[2,2,32,8,2048]{4,3,0,1,2:T(8,128)(2,1)} async-done(((bf16[2,2,32,8,2048]{4,3,0,1,2:T(8,128)(2,1)}), bf16[2,2,32,8,2048]{4,3,0,1,2:T(8,128)(2,1)}, u32[]{:S(2)}, u32[]{:S(2)}) %all-to-all-start.1) | async-done | bytes 4194336 | tf_op jit(solution)/shard_map/all_to_all | solution.py:87
  139.8 2.5 copy.69
  142.3 2.7 fusion.14
  145.0 2.7 fusion.15
  147.7 2.9 %subtract_bitcast_fusion = f32[2,2,128,2048]{2,3,1,0:T(8,128)S(1)} fusion(f32[2,2,2048,128]{3,2,1,0:T(8,128)S(1)} %fusion.14, bf16[2,2,2,128,2048]{4,3,2,1,0:T(8,128)(2,1)S(1)} %bitcast.160), kind=kOutput, calls=%fused_computation.11 | convolution fusion | flops 1612939264 | bytes 10485760 | tf_op jit(solution)/shard_map/kb,xsbc->xskc/dot_general | solution.py:31
  150.7 2.9 %add_bitcast_fusion = f32[2,2,128,2048]{2,3,1,0:T(8,128)S(1)} fusion(f32[2,2,2048,128]{3,2,1,0:T(8,128)S(1)} %fusion.15, bf16[2,2,2,128,2048]{4,3,2,1,0:T(8,128)(2,1)S(1)} %bitcast.161), kind=kOutput, calls=%fused_computation.10 | convolution fusion | flops 1612939264 | bytes 10485760 | tf_op jit(solution)/shard_map/kb,xsbc->xskc/dot_general | solution.py:31
  154.1 2.3 fusion.8
  156.4 2.1 fusion.12
  158.5 2.1 convolution_add_fusion
  160.7 2.5 fusion.16
  163.2 1.5 pad_maximum_fusion.1
  164.7 6.3 %copy.42 = bf16[2,2,128,2048]{3,1,0,2:T(2,128)(2,1)} copy(bf16[2,2,128,2048]{2,3,1,0:T(8,128)(2,1)} %pad_maximum_fusion.1) | data formatting | bytes 4194304 | tf_op jit(solution)/shard_map/stack | solution.py:98
  171.0 66.7 %all_to_all.54 = bf16[2,2,128,2048]{3,1,0,2:T(2,128)(2,1)S(1)} all-to-all(bf16[2,2,128,2048]{3,1,0,2:T(2,128)(2,1)} %copy.42), channel_id=1, replica_groups=mesh['seq'=16,'ch'=2] {'seq'}, dimensions={2} | all-to-all | bytes 4194304 | tf_op jit(solution)/shard_map/all_to_all | solution.py:101
  240.0 2.1 copy.44
  242.1 2.3 squeeze.13
  244.4 2.9 %fusion.56 = f32[16,8,2048]{2,0,1:T(8,128)} fusion(bf16[32,8,2048]{2,0,1:T(8,128)(2,1)} %squeeze.13), kind=kOutput, calls=%fused_computation.92 | convolution fusion | flops 100670464 | bytes 2097152 | tf_op jit(solution)/shard_map/ak,kbc->abc/dot_general | solution.py:31
  247.3 2.0 copy.45
  249.3 2.3 squeeze.14
  251.6 2.2 fusion.5
  254.1 17.8 %all_to_all.55 = bf16[16,8,2048]{2,1,0:T(8,128)(2,1)S(1)} all-to-all(bf16[16,8,2048]{2,1,0:T(8,128)(2,1)S(1)} %copy.46), channel_id=1, replica_groups=mesh['seq'=16,'ch'=2] {'seq'}, dimensions={0} | all-to-all | bytes 1048576 | tf_op jit(solution)/shard_map/all_to_all | solution.py:106
  273.2 2.4 psum.7
  275.7 2.8 multiply_convert_fusion
  (38 shorter events, 8.2 us)
Async XLA Ops:
  0.6 6.6 %copy-start.5 = (f32[3,3,2048]{2,1,0:T(4,128)S(1)}, f32[3,3,2048]{2,1,0:T(4,128)}, u32[]{:S(2)}) copy-start(f32[3,3,2048]{2,1,0:T(4,128)} %param.10) | copy-start | bytes 221188
  0.6 6.7 %copy-start.4 = (f32[128,2048]{1,0:T(8,128)S(1)}, f32[128,2048]{1,0:T(8,128)}, u32[]{:S(2)}) copy-start(f32[128,2048]{1,0:T(8,128)} %param.11) | copy-start | bytes 3145732
  0.7 8.1 %copy-start = (bf16[128,2048]{1,0:T(8,128)(2,1)S(1)}, bf16[128,2048]{1,0:T(8,128)(2,1)}, u32[]{:S(2)}) copy-start(bf16[128,2048]{1,0:T(8,128)(2,1)} %param.9) | copy-start | bytes 1572868
  0.7 8.1 %copy-start.1 = (bf16[128,2048]{1,0:T(8,128)(2,1)S(1)}, bf16[128,2048]{1,0:T(8,128)(2,1)}, u32[]{:S(2)}) copy-start(bf16[128,2048]{1,0:T(8,128)(2,1)} %param.8) | copy-start | bytes 1572868
  0.7 8.1 %copy-start.2 = (bf16[128,2048]{1,0:T(8,128)(2,1)S(1)}, bf16[128,2048]{1,0:T(8,128)(2,1)}, u32[]{:S(2)}) copy-start(bf16[128,2048]{1,0:T(8,128)(2,1)} %param.7) | copy-start | bytes 1572868
  2.4 6.4 %collective-permute-start = (bf16[3,2,2048]{2,1,0:T(2,128)(2,1)S(1)}, bf16[3,2,2048]{2,1,0:T(2,128)(2,1)S(1)}, u32[]{:S(2)}, u32[]{:S(2)}) collective-permute-start(bf16[3,2,2048]{2,1,0:T(2,128)(2,1)S(1)} %slice.74), channel_id=1, source_target_pairs={{0,2},{2,4},{4,6},{6,8},{8,10},{10,12},{12,14},{14,16},{16,18},{18... | collective-permute-start | bytes 73736 | tf_op jit(solution)/shard_map/ppermute | solution.py:17
  12.5 31.6 %all-to-all-start = ((bf16[2,1,128,2048]{3,0,1,2:T(2,128)(2,1)}), bf16[2,1,128,2048]{3,0,1,2:T(2,128)(2,1)}, u32[]{:S(2)}, u32[]{:S(2)}) async-start(bf16[2,1,128,2048]{3,0,1,2:T(2,128)(2,1)} %copy.33), calls=%async_computation | async-start | bytes 2097152 | tf_op jit(solution)/shard_map/all_to_all | solution.py:75
  56.0 83.7 %all-to-all-start.1 = ((bf16[2,2,32,8,2048]{4,3,0,1,2:T(8,128)(2,1)}), bf16[2,2,32,8,2048]{4,3,0,1,2:T(8,128)(2,1)}, u32[]{:S(2)}, u32[]{:S(2)}) async-start(bf16[2,2,32,8,2048]{4,3,0,1,2:T(8,128)(2,1)} %copy.37), calls=%async_computation.1 | async-start | bytes 8388608 | tf_op jit(solution)/shard_map/all_to_all | solution.py:87
  244.4 2.9 %copy-start.3 = (bf16[1,16,2,8,2048]{4,3,1,2,0:T(8,128)(2,1)S(1)}, bf16[1,16,2,8,2048]{4,3,1,2,0:T(8,128)(2,1)}, u32[]{:S(2)}) copy-start(bf16[1,16,2,8,2048]{4,3,1,2,0:T(8,128)(2,1)} %get-tuple-element.10) | copy-start | bytes 3145732
  251.6 20.3 %copy-start.6 = (f32[2048]{0:T(1024)S(1)}, f32[2048]{0:T(1024)}, u32[]{:S(2)}) copy-start(f32[2048]{0:T(1024)} %param.12) | copy-start | bytes 24580
  271.9 3.8 %copy-start.7 = (f32[2048]{0:T(1024)S(1)}, f32[2048]{0:T(1024)}, u32[]{:S(2)}) copy-start(f32[2048]{0:T(1024)} %param.13) | copy-start | bytes 24580
where the time goes:
time: 282 us; the launch traced here: 279 us
  waiting for transfers between devices  102 us (36%)
  blocking collectives  86.9 us (31%)
  matrix products  31.2 us (11%)
  local copies, waits for them, and re-layouts  28.2 us (10%)
  starting transfers between devices  19.2 us (7%)
  other arithmetic  10 us (4%)
    all_to_all x1, waiting for transfers between devices, shards(): lax.all_to_all(for_sending(spread), 'seq', split_axis=2, concat_axis=3, t...  77.5 us
    all_to_all x1, blocking collectives, shards(): lax.all_to_all(for_sending(spectra), 'seq', split_axis=2, concat_axis=1,...  66.7 us
    dot_general x12, matrix products, contract(): return jnp.einsum(pattern, table, values, precision=highest_precision)  31.2 us
    all_to_all x1, waiting for transfers between devices, shards(): lax.all_to_all(signals.astype(jnp.bfloat16), 'seq', split_axis=2, concat_...  23.2 us
    all_to_all x1, blocking collectives, shards(): lax.all_to_all(for_sending(returned), 'seq', split_axis=0, concat_axis=1,...  17.8 us
    all_to_all x1, starting transfers between devices, shards(): lax.all_to_all(signals.astype(jnp.bfloat16), 'seq', split_axis=2, concat_...  8.27 us
    another operation x1, local copies, waits for them, and re-layouts, shards(): jnp.stack([real_part * cosine - imag_part * sine, imag_part * cosine + re...  6.28 us
    all_to_all x1, starting transfers between devices, shards(): lax.all_to_all(for_sending(spread), 'seq', split_axis=2, concat_axis=3, t...  6.05 us
  transfers between devices with their start and end apart: 3, of which 3 were waited for; matrix products, arithmetic and copies ran while one was open for 0% of the time, Pallas kernels for 0%

commit v1 on v0

--- a/solution.py
+++ b/solution.py
@@ -1,11 +1,202 @@
+import functools
 import math
 
 import jax
 import jax.numpy as jnp
+import numpy as np
 from jax import lax
+from jax.experimental import pallas as pl
+from jax.experimental.pallas import tpu as pltpu
 from jax.sharding import PartitionSpec as P
 
 D = 4096
+RADIX = 16
+HALF = RADIX // 2
+LANES = 128
+MESH = pl.DeviceIdType.MESH
+
+
+def dft_tables(seq):
+    length = 2 * seq
+    inner = length // RADIX
+    tokens = np.arange(inner, dtype=np.int64)
+
+    def waves(freq):
+        angle = (freq[:, None] * tokens[None, :] % length) * (2.0 * math.pi / length)
+        return np.cos(angle), np.sin(angle)
+
+    full = []
+    for k1 in range(1, HALF):
+        c, s = waves(k1 + RADIX * np.arange(inner, dtype=np.int64))
+        full.append(np.block([[c, s], [-s, c]]))
+    real = []
+    for k1 in (0, HALF):
+        c, s = waves(k1 + RADIX * np.arange(inner // 2, dtype=np.int64))
+        table = np.concatenate([c, -s])
+        if k1 == 0:
+            table[inner // 2] = np.cos(math.pi * tokens)
+        real.append(table)
+
+    def split(table):
+        high = table.astype(jnp.bfloat16)
+        low = (table - high.astype(np.float64)).astype(jnp.bfloat16)
+        return np.concatenate([high, low], axis=-1)
+
+    full, real = np.stack(full), np.stack(real)
+    turn = lambda a: np.swapaxes(a, 1, 2)
+    return split(full), split(real), split(turn(full)), split(turn(real))
+
+
+def turned(cr, ci, a):
+    return (cr * a[0] - ci * a[1], cr * a[1] + ci * a[0])
+
+
+def unit(power):
+    angle = 2.0 * math.pi * power / RADIX
+    return math.cos(angle), math.sin(angle)
+
+
+def block_dft(x):
+    s = math.sqrt(0.5)
+    a = [x[n] + x[n + 4] for n in range(4)]
+    b = [x[n] - x[n + 4] for n in range(4)]
+    out = {}
+    e, o = a[0] + a[2], a[1] + a[3]
+    out[0], out[8] = e + o, e - o
+    out[4] = (a[0] - a[2], a[3] - a[1])
+    d, m = s * (b[1] - b[3]), s * (b[1] + b[3])
+    out[2] = (b[0] + d, -b[2] - m)
+    out[6] = (b[0] - d, b[2] - m)
+    for first, sign in ((1, -1.0), (3, 1.0)):
+        t = [(x[0], sign * x[4])]
+        for n in range(1, 4):
+            cr, ci = unit(-first * n)
+            t.append(turned(cr, ci, (x[n], sign * x[n + 4])))
+        er, ei = t[0][0] + t[2][0], t[0][1] + t[2][1]
+        dr, di = t[0][0] - t[2][0], t[0][1] - t[2][1]
+        fr, fi = t[1][0] + t[3][0], t[1][1] + t[3][1]
+        gr, gi = t[1][0] - t[3][0], t[1][1] - t[3][1]
+        out[first] = (er + fr, ei + fi)
+        out[first + 4] = (dr + gi, di - gr)
+    return out
+
+
+def block_idft(u):
+    s = math.sqrt(0.5)
+    p, m = u[0] + u[8], u[0] - u[8]
+    a = [p + u[4][0], m - u[4][1], p - u[4][0], m + u[4][1]]
+    b = [
+        u[2][0] + u[6][0],
+        s * ((u[2][0] - u[2][1]) - (u[6][0] + u[6][1])),
+        u[6][1] - u[2][1],
+        s * ((u[6][0] - u[6][1]) - (u[2][0] + u[2][1])),
+    ]
+    out = [None] * HALF
+    for n in range(4):
+        low, high = a[n] + b[n], a[n] - b[n]
+        for first, sign in ((1, -1.0), (3, 1.0)):
+            v, w = u[first], u[first + 4]
+            if n == 0:
+                v = (v[0] + w[0], v[1] + w[1])
+            elif n == 1:
+                v = (v[0] - w[1], v[1] + w[0])
+            elif n == 2:
+                v = (v[0] - w[0], v[1] - w[1])
+            else:
+                v = (v[0] + w[1], v[1] - w[0])
+            q = turned(*unit(first * n), v)
+            low, high = low + q[0], high + sign * q[1]
+        out[n], out[n + 4] = low, high
+    return out
+
+
+CHUNK = 32
+
+
+def spread_blocks(inner, load, y_full, y_real):
+    def step(i, carry):
+        start = pl.multiple_of(i * CHUNK, CHUNK)
+        rows = pl.ds(start, CHUNK)
+        out = block_dft([load(n, start) for n in range(HALF)])
+        y_real[0, rows, :] = out[0].astype(jnp.bfloat16)
+        y_real[1, rows, :] = out[HALF].astype(jnp.bfloat16)
+        lower = pl.ds(pl.multiple_of(inner + start, CHUNK), CHUNK)
+        for k in range(1, HALF):
+            y_full[k - 1, rows, :] = out[k][0].astype(jnp.bfloat16)
+            y_full[k - 1, lower, :] = out[k][1].astype(jnp.bfloat16)
+        return carry
+
+    lax.fori_loop(0, inner // CHUNK, step, 0)
+
+
+def both(table, values):
+    half = table.shape[1] // 2
+    first = jnp.dot(table[:, :half], values, preferred_element_type=jnp.float32)
+    return first + jnp.dot(table[:, half:], values, preferred_element_type=jnp.float32)
+
+
+def filter_spectrum(f_full, f_real, y_full, y_real, h_full, h_real):
+    for i in range(2):
+        h_real[i] = both(f_real[i], y_real[i])
+
+    def step(k, carry):
+        h_full[k] = both(f_full[k], y_full[k])
+        return carry
+
+    lax.fori_loop(0, HALF - 1, step, 0)
+
+
+def filtered(inner, f_full, f_real, g_full, g_real, y_full, y_real, h_full, h_real):
+    length = inner * RADIX
+
+    def product(a, b, size):
+        ar, ai, br, bi = a[:size], a[size:], b[:size], b[size:]
+        return ar * br - ai * bi, ar * bi + ai * br
+
+    for i in range(2):
+        half = inner // 2
+        a, b = both(f_real[i], y_real[i]), h_real[i]
+        pr, pi = product(a, b, half)
+        pr, pi = pr * (2.0 / length), pi * (2.0 / length)
+        if i == 0:
+            top = lax.broadcasted_iota(jnp.int32, pr.shape, 0) == 0
+            pr = jnp.where(top, a[:half] * b[:half] * (1.0 / length), pr)
+            pi = jnp.where(top, a[half:] * b[half:] * (1.0 / length), pi)
+        z = jnp.concatenate([pr, pi]).astype(jnp.bfloat16)
+        h_real[i] = both(g_real[i], z)
+
+    def step(k, carry):
+        pr, pi = product(both(f_full[k], y_full[k]), h_full[k], inner)
+        z = (jnp.concatenate([pr, pi]) * (2.0 / length)).astype(jnp.bfloat16)
+        h_full[k] = both(g_full[k], z)
+        return carry
+
+    lax.fori_loop(0, HALF - 1, step, 0)
+
+
+def gather_blocks(inner, h_full, h_real, store):
+    def step(i, carry):
+        start = pl.multiple_of(i * CHUNK, CHUNK)
+        rows = pl.ds(start, CHUNK)
+        lower = pl.ds(pl.multiple_of(inner + start, CHUNK), CHUNK)
+        u = {0: h_real[0, rows, :], HALF: h_real[1, rows, :]}
+        for k in range(1, HALF):
+            u[k] = (h_full[k - 1, rows, :], h_full[k - 1, lower, :])
+        for n, block in enumerate(block_idft(u)):
+            store(n, start, block.astype(jnp.bfloat16))
+        return carry
+
+    lax.fori_loop(0, inner // CHUNK, step, 0)
+
+
+def spectrum_scratch(inner):
+    wide = (HALF - 1, 2 * inner, LANES)
+    return [
+        pltpu.VMEM(wide, jnp.bfloat16),
+        pltpu.VMEM((2, inner, LANES), jnp.bfloat16),
+        pltpu.VMEM(wide, jnp.float32),
+        pltpu.VMEM((2, inner, LANES), jnp.float32),
+    ]
 
 
 highest_precision = lax.Precision.HIGHEST
@@ -113,9 +304,69 @@
     return (mixed.astype(jnp.bfloat16), normed)
 
 
+def conv_kernel(inner, x_ref, f_full, f_real, g_full, g_real, o_ref, y_full, y_real, h_full, h_real):
+    def load(which, n, start):
+        rows = pl.ds(pl.multiple_of(n * inner + start, CHUNK), CHUNK)
+        return x_ref[which, rows, :].astype(jnp.float32)
+
+    def store(n, start, block):
+        o_ref[pl.ds(pl.multiple_of(n * inner + start, CHUNK), CHUNK), :] = block
+
+    spread_blocks(inner, functools.partial(load, 1), y_full, y_real)
+    filter_spectrum(f_full, f_real, y_full, y_real, h_full, h_real)
+    spread_blocks(inner, functools.partial(load, 0), y_full, y_real)
+    filtered(inner, f_full, f_real, g_full, g_real, y_full, y_real, h_full, h_real)
+    gather_blocks(inner, h_full, h_real, store)
+
+
+def long_convolution(signals, seq):
+    inner = seq // HALF
+    tables = [jnp.asarray(t) for t in dft_tables(seq)]
+    return pl.pallas_call(
+        functools.partial(conv_kernel, inner),
+        out_shape=jax.ShapeDtypeStruct((seq, LANES), jnp.bfloat16),
+        in_specs=[pl.BlockSpec(memory_space=pltpu.VMEM)] * 5,
+        out_specs=pl.BlockSpec(memory_space=pltpu.VMEM),
+        scratch_shapes=spectrum_scratch(inner),
+        compiler_params=pltpu.CompilerParams(vmem_limit_bytes=48 * 2**20),
+    )(signals, *tables)
+
+
+def channel_shards(q_proj, k_proj, v_proj, feat_filter, long_filter, skip_bias, norm_gain):
+    rows = q_proj.shape[0]
+    taps = feat_filter.shape[1]
+    seq = rows * lax.axis_size("seq")
+    stacked = jnp.stack([q_proj, k_proj, v_proj])
+    previous = shifted(stacked[:, rows - (taps - 1) :, :], "seq", 1)
+    extended = jnp.concatenate([previous, stacked], axis=1)
+    featured = jnp.zeros(stacked.shape, jnp.float32)
+    for offset in range(taps):
+        window = extended[:, taps - 1 - offset : taps - 1 - offset + rows, :]
+        featured = featured + feat_filter[:, offset, None, :] * window.astype(jnp.float32)
+    query = featured[0]
+    gated = featured[1] * featured[2]
+    signals = jnp.stack([gated, long_filter]).astype(jnp.bfloat16)
+    pieces = lax.all_to_all(signals, "seq", split_axis=2, concat_axis=1, tiled=True)
+    returned = long_convolution(pieces, seq)
+    long_conv = lax.all_to_all(returned, "seq", split_axis=0, concat_axis=1, tiled=True)
+    mixed = query * (long_conv.astype(jnp.float32) + skip_bias * gated)
+    squares = lax.psum(jnp.sum(mixed * mixed, axis=1), "ch")
+    scale = lax.rsqrt(squares / D + 1e-05)
+    normed = (mixed * scale[:, None] * norm_gain).astype(jnp.bfloat16)
+    return (mixed.astype(jnp.bfloat16), normed)
+
+
 def solution(mesh):
+    def layer(*arrays):
+        rows, channels = arrays[0].shape
+        seq = rows * mesh.shape["seq"]
+        whole_lanes = channels == LANES * mesh.shape["seq"]
+        if whole_lanes and seq % (HALF * 256) == 0 and seq <= 2048:
+            return channel_shards(*arrays)
+        return shards(*arrays)
+
     return jax.shard_map(
-        shards,
+        layer,
         mesh=mesh,
         in_specs=(
             P("seq", "ch"),

time: 282 us -> 90.5 us (0.32); the launches traced: 279 us -> 90.2 us
  waiting for transfers between devices: 102 us -> 1.3 us
  blocking collectives: 86.9 us -> 53 us
  matrix products: 31.2 us -> 0 us
  local copies, waits for them, and re-layouts: 28.2 us -> 5.02 us
  Pallas kernels: 0 us -> 20.3 us
  starting transfers between devices: 19.2 us -> 4.84 us
  other arithmetic: 10 us -> 4.88 us
    all_to_all x2 -> x0, waiting for transfers between devices: 101 us -> none  [the longest x1 77.5 us: shards(): lax.all_to_all(for_sending(spread), 'seq', split_axis=2, concat_axis=3, t...]
    all_to_all x2, blocking collectives: 84.5 us -> 50.5 us  [the longest x1 32.9 us: channel_shards(): lax.all_to_all(signals, 'seq', split_axis=2, concat_axis=1, tiled=True)]
    dot_general x12 -> x0, matrix products: 31.2 us -> none  [contract(): return jnp.einsum(pattern, table, values, precision=highest_precision)]
    pallas_call x0 -> x1, Pallas kernels: none -> 20.3 us  [long_convolution(): pl.pallas_call(functools.partial(conv_kernel, inner), out_shape=jax.Shape...]
    all_to_all x2 -> x0, starting transfers between devices: 14.3 us -> none  [the longest x1 8.27 us: shards(): lax.all_to_all(signals.astype(jnp.bfloat16), 'seq', split_axis=2, concat_...]
    another operation x3 -> x1, local copies, waits for them, and re-layouts: 12.6 us -> 0.79 us  [channel_shards(): signals = jnp.stack([gated, long_filter]).astype(jnp.bfloat16)]
    slice x5 -> x2, local copies, waits for them, and re-layouts: 5.37 us -> 0.08 us  [the longest x1 0.05 us: channel_shards(): feat_filter[:, offset, None, :] * window.astype(jnp.float32)]
    squeeze x2 -> x0, local copies, waits for them, and re-layouts: 4.51 us -> none  [the longest x1 2.25 us: shards(): pieces[1]]
  transfers between devices with their start and end apart: 3 -> 1, of which waited for: 3 -> 1; matrix products, arithmetic and copies ran while one was open for 0% -> 0% of each run, Pallas kernels for 0% -> 0%
where the time goes in v1:
time: 90.5 us; the launch traced here: 90.2 us
  blocking collectives  53 us (59%)
  Pallas kernels  20.3 us (22%)
  local copies, waits for them, and re-layouts  5.02 us (6%)
  other arithmetic  4.88 us (5%)
  starting transfers between devices  4.84 us (5%)
  waiting for transfers between devices  1.3 us (1%)
    all_to_all x1, blocking collectives, channel_shards(): lax.all_to_all(signals, 'seq', split_axis=2, concat_axis=1, tiled=True)  32.9 us
    pallas_call x1, Pallas kernels, long_convolution(): pl.pallas_call(functools.partial(conv_kernel, inner), out_shape=jax.Shape...  20.3 us
    all_to_all x1, blocking collectives, channel_shards(): lax.all_to_all(returned, 'seq', split_axis=0, concat_axis=1, tiled=True)  17.7 us
    ppermute x1, starting transfers between devices, shifted(): return lax.ppermute(block, axis, route)  4.84 us
    all_to_all x1, local copies, waits for them, and re-layouts, channel_shards(): lax.all_to_all(signals, 'seq', split_axis=2, concat_axis=1, tiled=True)  2.54 us
    psum x1, blocking collectives, channel_shards(): squares = lax.psum(jnp.sum(mixed * mixed, axis=1), 'ch')  2.47 us
  transfers between devices with their start and end apart: 1, of which 1 were waited for; matrix products, arithmetic and copies ran while one was open for 0% of the time, Pallas kernels for 0%

profile of v1, /device:TPU:0, one launch (start us, length us, event | category | flops | bytes accessed | tf_op | source)
XLA Modules:
  0.0 90.2 jit_solution(5441457821625681873)
XLA Ops:
  0.6 0.0 copy-start.6
  0.6 0.0 copy-start.5
  0.7 0.0 copy-start.4
  0.7 0.0 copy-start.8
  0.7 0.0 copy-start.7
  0.7 1.7 %pad_maximum_fusion = bf16[3,128,2048]{2,1,0:T(8,128)(2,1)S(1)} fusion(bf16[1,128,2048]{2,1,0:T(8,128)(2,1)} %bitcast.38, bf16[1,128,2048]{2,1,0:T(8,128)(2,1)} %bitcast.41, bf16[1,128,2048]{2,1,0:T(8,128)(2,1)} %bitcast.44), kind=kLoop, calls=%fused_computation.2 | loop fusion | flops 1572864 | bytes 3145728 | tf_op jit(solution)/shard_map/stack | solution.py:339
  2.4 4.8 %collective-permute-start = (bf16[3,2,2048]{2,1,0:T(2,128)(2,1)S(1)}, bf16[3,2,2048]{2,1,0:T(2,128)(2,1)S(1)}, u32[]{:S(2)}, u32[]{:S(2)}) collective-permute-start(bf16[3,2,2048]{2,1,0:T(2,128)(2,1)S(1)} %slice.36), channel_id=1, source_target_pairs={{0,2},{2,4},{4,6},{6,8},{8,10},{10,12},{12,14},{14,16},{16,18},{18... | collective-permute-start | bytes 73736 | tf_op jit(solution)/shard_map/ppermute | solution.py:208
  7.3 0.0 copy-done.8
  7.3 0.1 fusion.3
  7.3 0.0 copy-done.7
  7.3 0.1 convert_bitcast_fusion.1
  7.5 1.3 %collective-permute-done = bf16[3,2,2048]{2,1,0:T(2,128)(2,1)S(1)} collective-permute-done((bf16[3,2,2048]{2,1,0:T(2,128)(2,1)S(1)}, bf16[3,2,2048]{2,1,0:T(2,128)(2,1)S(1)}, u32[]{:S(2)}, u32[]{:S(2)}) %collective-permute-start) | collective-permute-done | bytes 24608 | tf_op jit(solution)/shard_map/ppermute | solution.py:208
  8.8 0.0 copy-done.6
  8.8 0.0 copy-done.5
  8.8 0.5 maximum_maximum_fusion
  9.2 0.9 %multiply_add_fusion = f32[3,128,2048]{2,1,0:T(8,128)S(1)} fusion(bf16[3,130,2048]{2,1,0:T(8,128)(2,1)S(1)} %maximum_maximum_fusion, f32[3,2048]{1,0:T(4,128)S(1)} %get-tuple-element.11, f32[3,2048]{1,0:T(4,128)S(1)} %get-tuple-element.12, f32[3,2048]{1,0:T(4,128)S(1)} %bitcast.48, bf16[1,128,2048]{2,1,0:T(8,128)(2,1)S(1)} %bitcast.40, ...), kind=kLoop, calls=%fused_computation | loop fusion | flops 7864320 | bytes 7938048 | tf_op jit(solution)/shard_map/add | solution.py:345
  10.2 0.1 fusion.1
  10.3 1.5 %copy-done.2 = f32[3,128,2048]{2,1,0:T(8,128)} copy-done((f32[3,128,2048]{2,1,0:T(8,128)}, f32[3,128,2048]{2,1,0:T(8,128)S(1)}, u32[]{:S(2)}) %copy-start.2) | copy-done | bytes 3145752
  11.8 0.1 pad_maximum_fusion.1
  11.9 0.0 copy-start
  11.9 0.0 copy-start.1
  11.9 0.8 copy.27
  12.7 32.9 %all_to_all.31 = bf16[2,128,2048]{1,0,2:T(2,128)(2,1)} all-to-all(bf16[2,128,2048]{1,0,2:T(2,128)(2,1)S(1)} %copy.27), channel_id=1, replica_groups=mesh['seq'=16,'ch'=2] {'seq'}, dimensions={2} | all-to-all | bytes 2097152 | tf_op jit(solution)/shard_map/all_to_all | solution.py:349
  45.6 2.5 %copy.28 = bf16[2,128,16,128]{3,1,2,0:T(8,128)(2,1)S(1)} copy(bf16[2,128,16,128]{1,0,3,2:T(2,128)(2,1)} %bitcast.47) | data formatting | bytes 2097152 | tf_op jit(solution)/shard_map/all_to_all | solution.py:349
  48.2 0.0 copy-start.9
  48.2 20.3 %shard_map.122 = bf16[2048,128]{1,0:T(8,128)(2,1)S(1)} custom-call(bf16[2,2048,128]{2,1,0:T(8,128)(2,1)S(1)} %bitcast.36, bf16[7,512,1024]{2,1,0:T(8,128)(2,1)} %constant.15.clone.f_full, bf16[2,256,512]{2,1,0:T(8,128)(2,1)S(1)} %copy-done, bf16[7,512,1024]{2,1,0:T(8,128)(2,1)} %constant.17.clone.g_full, bf16[2,256,512]{2,1,0:T(8,128)(2,1)S(1)} %copy-done.1), custom_call_target="tpu_custom_call" | custom-call | tf_op jit(solution)/shard_map/pallas_call | solution.py:325
  68.5 0.0 copy-start.10
  68.5 17.7 %all_to_all.32 = bf16[16,128,128]{2,1,0:T(8,128)(2,1)S(1)} all-to-all(bf16[16,128,128]{2,1,0:T(8,128)(2,1)S(1)} %bitcast.37), channel_id=1, replica_groups=mesh['seq'=16,'ch'=2] {'seq'}, dimensions={0} | all-to-all | bytes 1048576 | tf_op jit(solution)/shard_map/all_to_all | solution.py:351
  86.2 0.0 copy-done.3
  86.2 0.4 multiply_reduce_fusion
  86.6 2.5 %psum.7 = f32[128]{0:T(128)S(1)} all-reduce(f32[128]{0:T(128)S(1)} %get-tuple-element.4), channel_id=1, replica_groups=mesh['seq'=16,'ch'=2] {'ch'}, use_global_device_ids=true, to_apply=%region_1.0 | all-reduce | flops 128 | bytes 1024 | tf_op jit(solution)/shard_map/psum | solution.py:353
  89.1 1.1 %multiply_convert_fusion = (bf16[128,2048]{1,0:T(8,128)(2,1)}, bf16[128,2048]{1,0:T(8,128)(2,1)}) fusion(f32[128,2048]{1,0:T(8,128)S(1)} %get-tuple-element.5, f32[2048]{0:T(1024)S(1)} %copy-done.10, f32[128]{0:T(128)S(1)} %add_rsqrt_fusion), kind=kLoop, calls=%fused_computation.10 | loop fusion | flops 1048576 | bytes 2105856 | tf_op jit(solution)/shard_map/convert_element_type | solution.py:355
  (11 shorter events, 0.1 us)
Async XLA Ops:
  0.6 8.1 %copy-start.6 = (bf16[128,2048]{1,0:T(8,128)(2,1)S(1)}, bf16[128,2048]{1,0:T(8,128)(2,1)}, u32[]{:S(2)}) copy-start(bf16[128,2048]{1,0:T(8,128)(2,1)} %param.11) | copy-start | bytes 1572868
  0.6 8.1 %copy-start.5 = (bf16[128,2048]{1,0:T(8,128)(2,1)S(1)}, bf16[128,2048]{1,0:T(8,128)(2,1)}, u32[]{:S(2)}) copy-start(bf16[128,2048]{1,0:T(8,128)(2,1)} %param.12) | copy-start | bytes 1572868
  0.7 8.1 %copy-start.4 = (bf16[128,2048]{1,0:T(8,128)(2,1)S(1)}, bf16[128,2048]{1,0:T(8,128)(2,1)}, u32[]{:S(2)}) copy-start(bf16[128,2048]{1,0:T(8,128)(2,1)} %param.13) | copy-start | bytes 1572868
  0.7 6.6 %copy-start.8 = (f32[3,3,2048]{2,1,0:T(4,128)S(1)}, f32[3,3,2048]{2,1,0:T(4,128)}, u32[]{:S(2)}) copy-start(f32[3,3,2048]{2,1,0:T(4,128)} %param.14) | copy-start | bytes 221188
  0.7 6.7 %copy-start.7 = (f32[128,2048]{1,0:T(8,128)S(1)}, f32[128,2048]{1,0:T(8,128)}, u32[]{:S(2)}) copy-start(f32[128,2048]{1,0:T(8,128)} %param.15) | copy-start | bytes 3145732
  2.4 6.4 %collective-permute-start = (bf16[3,2,2048]{2,1,0:T(2,128)(2,1)S(1)}, bf16[3,2,2048]{2,1,0:T(2,128)(2,1)S(1)}, u32[]{:S(2)}, u32[]{:S(2)}) collective-permute-start(bf16[3,2,2048]{2,1,0:T(2,128)(2,1)S(1)} %slice.36), channel_id=1, source_target_pairs={{0,2},{2,4},{4,6},{6,8},{8,10},{10,12},{12,14},{14,16},{16,18},{18... | collective-permute-start | bytes 73736 | tf_op jit(solution)/shard_map/ppermute | solution.py:208
  10.2 1.6 %copy-start.2 = (f32[3,128,2048]{2,1,0:T(8,128)}, f32[3,128,2048]{2,1,0:T(8,128)S(1)}, u32[]{:S(2)}) copy-start(f32[3,128,2048]{2,1,0:T(8,128)S(1)} %multiply_add_fusion) | copy-start | bytes 9437188
  11.9 36.2 %copy-start = (bf16[2,256,512]{2,1,0:T(8,128)(2,1)S(1)}, bf16[2,256,512]{2,1,0:T(8,128)(2,1)}, u32[]{:S(2)}) copy-start(bf16[2,256,512]{2,1,0:T(8,128)(2,1)} %constant.16.clone.f_real) | copy-start | bytes 1572868
  11.9 36.2 %copy-start.1 = (bf16[2,256,512]{2,1,0:T(8,128)(2,1)S(1)}, bf16[2,256,512]{2,1,0:T(8,128)(2,1)}, u32[]{:S(2)}) copy-start(bf16[2,256,512]{2,1,0:T(8,128)(2,1)} %constant.18.clone.g_real) | copy-start | bytes 1572868
  48.2 38.0 %copy-start.3 = (f32[3,128,2048]{2,1,0:T(8,128)S(1)}, f32[3,128,2048]{2,1,0:T(8,128)}, u32[]{:S(2)}) copy-start(f32[3,128,2048]{2,1,0:T(8,128)} %copy-done.2) | copy-start | bytes 9437188
  48.2 38.0 %copy-start.9 = (f32[2048]{0:T(1024)S(1)}, f32[2048]{0:T(1024)}, u32[]{:S(2)}) copy-start(f32[2048]{0:T(1024)} %param.16) | copy-start | bytes 24580
  68.5 20.6 %copy-start.10 = (f32[2048]{0:T(1024)S(1)}, f32[2048]{0:T(1024)}, u32[]{:S(2)}) copy-start(f32[2048]{0:T(1024)} %param.17) | copy-start | bytes 24580

commit v2 on v1

--- a/solution.py
+++ b/solution.py
@@ -304,64 +304,255 @@
     return (mixed.astype(jnp.bfloat16), normed)
 
 
-def conv_kernel(inner, x_ref, f_full, f_real, g_full, g_real, o_ref, y_full, y_real, h_full, h_real):
-    def load(which, n, start):
-        rows = pl.ds(pl.multiple_of(n * inner + start, CHUNK), CHUNK)
-        return x_ref[which, rows, :].astype(jnp.float32)
-
-    def store(n, start, block):
-        o_ref[pl.ds(pl.multiple_of(n * inner + start, CHUNK), CHUNK), :] = block
-
-    spread_blocks(inner, functools.partial(load, 1), y_full, y_real)
+def mixer_kernel(
+    n, inner,
+    q_hbm, k_hbm, v_hbm, filter_hbm, f_full_hbm, f_real_hbm, g_full_hbm, g_real_hbm,
+    feat_ref, skip_ref, gain_ref,
+    mixed_ref, normed_ref,
+    q_ref, k_ref, v_ref, filter_ref, f_full, f_real, g_full, g_real,
+    tails, send_f, send_g, send_y, recv_f, recv_g, recv_y, query, gated, sums, other_sums,
+    y_full, y_real, h_full, h_real,
+    local_sem, tail_send, tail_recv, f_send, f_recv, g_send, g_recv, y_send, y_recv, sum_sem,
+):
+    me = lax.axis_index("seq")
+    core = lax.axis_index("ch")
+    other = 1 - core
+    rows = q_ref.shape[0]
+    after = lax.rem(me + 1, n)
+
+    def at(block):
+        return pl.ds(pl.multiple_of(block * rows, rows), rows)
+
+    def lanes(block):
+        return pl.ds(pl.multiple_of(block * LANES, LANES), LANES)
+
+    def partner(j):
+        offset = n // 2 + ((j + 1) // 2) * (2 * (j % 2) - 1)
+        return lax.rem(me + offset, n)
+
+    loads = [
+        pltpu.make_async_copy(source, target, local_sem.at[i])
+        for i, (source, target) in enumerate([
+            (filter_hbm, filter_ref), (k_hbm, k_ref), (v_hbm, v_ref), (q_hbm, q_ref),
+            (f_real_hbm, f_real), (f_full_hbm, f_full), (g_real_hbm, g_real), (g_full_hbm, g_full),
+        ])
+    ]
+    for load in loads:
+        load.start()
+
+    barrier = pltpu.get_barrier_semaphore()
+
+    def greet(j, carry):
+        pl.semaphore_signal(
+            barrier, inc=1, device_id=(partner(j), core), device_id_type=MESH
+        )
+        return carry
+
+    lax.fori_loop(0, n - 1, greet, 0)
+    pl.semaphore_signal(barrier, inc=1, device_id=(me, other), device_id_type=MESH)
+
+    loads[0].wait()
+
+    def narrow(j, carry):
+        send_f[at(j), :] = filter_ref[:, lanes(j)].astype(jnp.bfloat16)
+        return carry
+
+    lax.fori_loop(0, n, narrow, 0)
+    recv_f[at(me), :] = send_f[at(me), :]
+    for load in loads[1:4]:
+        load.wait()
+    pl.semaphore_wait(barrier, n)
+
+    def tail_copy(i, ref):
+        return pltpu.make_async_remote_copy(
+            src_ref=ref.at[pl.ds(rows - 16, 16), :],
+            dst_ref=tails.at[i],
+            send_sem=tail_send.at[i],
+            recv_sem=tail_recv.at[i],
+            device_id=(after, core),
+            device_id_type=MESH,
+        )
+
+    tail_copies = [tail_copy(i, ref) for i, ref in enumerate((k_ref, v_ref, q_ref))]
+    for copy in tail_copies:
+        copy.start()
+
+    def exchange(source, target, send_sem, recv_sem):
+        def to(peer):
+            return pltpu.make_async_remote_copy(
+                src_ref=source.at[at(peer), :],
+                dst_ref=target.at[at(me), :],
+                send_sem=send_sem.at[peer],
+                recv_sem=recv_sem.at[me],
+                device_id=(peer, core),
+                device_id_type=MESH,
+            )
+
+        def come(peer):
+            return pltpu.make_async_remote_copy(
+                src_ref=source.at[at(peer), :],
+                dst_ref=target.at[at(peer), :],
+                send_sem=send_sem.at[peer],
+                recv_sem=recv_sem.at[peer],
+                device_id=(peer, core),
+                device_id_type=MESH,
+            )
+
+        def start(j, carry):
+            to(partner(j)).start()
+            return carry
+
+        def arrive(j, carry):
+            come(partner(n - 2 - j)).wait_recv()
+            return carry
+
+        def leave(j, carry):
+            to(partner(j)).wait_send()
+            return carry
+
+        return (
+            lambda: lax.fori_loop(0, n - 1, start, 0),
+            lambda: lax.fori_loop(0, n - 1, arrive, 0),
+            lambda: lax.fori_loop(0, n - 1, leave, 0),
+        )
+
+    start_f, arrive_f, leave_f = exchange(send_f, recv_f, f_send, f_recv)
+    start_g, arrive_g, leave_g = exchange(send_g, recv_g, g_send, g_recv)
+    start_y, arrive_y, leave_y = exchange(send_y, recv_y, y_send, y_recv)
+    start_f()
+
+    first = me == 0
+
+    def featured(stream, tail, ref, j):
+        columns = lanes(j)
+        before = tails[tail, :, columns].astype(jnp.float32)
+        before = jnp.where(first, 0.0, before)
+        window = jnp.concatenate([before, ref[:, columns].astype(jnp.float32)])
+        total = feat_ref[3 * stream, :, columns] * window[16:]
+        for tap in (1, 2):
+            moved = pltpu.roll(window, tap, 0)[16:]
+            total = total + feat_ref[3 * stream + tap, :, columns] * moved
+        return total
+
+    for copy in tail_copies[:2]:
+        copy.wait()
+
+    def gate(j, carry):
+        value = featured(1, 0, k_ref, j) * featured(2, 1, v_ref, j)
+        gated[at(j), :] = value
+        send_g[at(j), :] = value.astype(jnp.bfloat16)
+        return carry
+
+    lax.fori_loop(0, n, gate, 0)
+    start_g()
+    recv_g[at(me), :] = send_g[at(me), :]
+    tail_copies[2].wait()
+
+    def ask(j, carry):
+        query[at(j), :] = featured(0, 2, q_ref, j)
+        return carry
+
+    lax.fori_loop(0, n, ask, 0)
+
+    def block_of(ref):
+        def load(block, start):
+            where = pl.ds(pl.multiple_of(block * inner + start, CHUNK), CHUNK)
+            return ref[where, :].astype(jnp.float32)
+
+        return load
+
+    def store(block, start, value):
+        send_y[pl.ds(pl.multiple_of(block * inner + start, CHUNK), CHUNK), :] = value
+
+    for load in loads[4:]:
+        load.wait()
+    arrive_f()
+    spread_blocks(inner, block_of(recv_f), y_full, y_real)
     filter_spectrum(f_full, f_real, y_full, y_real, h_full, h_real)
-    spread_blocks(inner, functools.partial(load, 0), y_full, y_real)
+    arrive_g()
+    spread_blocks(inner, block_of(recv_g), y_full, y_real)
     filtered(inner, f_full, f_real, g_full, g_real, y_full, y_real, h_full, h_real)
     gather_blocks(inner, h_full, h_real, store)
-
-
-def long_convolution(signals, seq):
+    start_y()
+    recv_y[at(me), :] = send_y[at(me), :]
+    leave_f()
+    leave_g()
+    arrive_y()
+
+    def mix(j, carry):
+        conv = recv_y[at(j), :].astype(jnp.float32)
+        mixed = query[at(j), :] * (conv + skip_ref[:, lanes(j)] * gated[at(j), :])
+        query[at(j), :] = mixed
+        mixed_ref[:, lanes(j)] = mixed.astype(jnp.bfloat16)
+        return carry + mixed * mixed
+
+    squares = lax.fori_loop(0, n, mix, jnp.zeros((rows, LANES), jnp.float32))
+    sums[...] = squares
+    sum_copy = pltpu.make_async_remote_copy(
+        src_ref=sums,
+        dst_ref=other_sums,
+        send_sem=sum_sem.at[0],
+        recv_sem=sum_sem.at[1],
+        device_id=(me, other),
+        device_id_type=MESH,
+    )
+    sum_copy.start()
+    leave_y()
+    sum_copy.wait()
+    total = jnp.sum(sums[...] + other_sums[...], axis=1, keepdims=True)
+    scale = lax.rsqrt(total / D + 1e-05)
+
+    def norm(j, carry):
+        value = query[at(j), :] * scale * gain_ref[:, lanes(j)]
+        normed_ref[:, lanes(j)] = value.astype(jnp.bfloat16)
+        return carry
+
+    lax.fori_loop(0, n, norm, 0)
+
+
+def channel_shards(q_proj, k_proj, v_proj, feat_filter, long_filter, skip_bias, norm_gain):
+    rows, channels = q_proj.shape
+    n = lax.axis_size("seq")
+    seq = rows * n
     inner = seq // HALF
     tables = [jnp.asarray(t) for t in dft_tables(seq)]
-    return pl.pallas_call(
-        functools.partial(conv_kernel, inner),
-        out_shape=jax.ShapeDtypeStruct((seq, LANES), jnp.bfloat16),
-        in_specs=[pl.BlockSpec(memory_space=pltpu.VMEM)] * 5,
-        out_specs=pl.BlockSpec(memory_space=pltpu.VMEM),
-        scratch_shapes=spectrum_scratch(inner),
-        compiler_params=pltpu.CompilerParams(vmem_limit_bytes=48 * 2**20),
-    )(signals, *tables)
-
-
-def channel_shards(q_proj, k_proj, v_proj, feat_filter, long_filter, skip_bias, norm_gain):
-    rows = q_proj.shape[0]
-    taps = feat_filter.shape[1]
-    seq = rows * lax.axis_size("seq")
-    stacked = jnp.stack([q_proj, k_proj, v_proj])
-    previous = shifted(stacked[:, rows - (taps - 1) :, :], "seq", 1)
-    extended = jnp.concatenate([previous, stacked], axis=1)
-    featured = jnp.zeros(stacked.shape, jnp.float32)
-    for offset in range(taps):
-        window = extended[:, taps - 1 - offset : taps - 1 - offset + rows, :]
-        featured = featured + feat_filter[:, offset, None, :] * window.astype(jnp.float32)
-    query = featured[0]
-    gated = featured[1] * featured[2]
-    signals = jnp.stack([gated, long_filter]).astype(jnp.bfloat16)
-    pieces = lax.all_to_all(signals, "seq", split_axis=2, concat_axis=1, tiled=True)
-    returned = long_convolution(pieces, seq)
-    long_conv = lax.all_to_all(returned, "seq", split_axis=0, concat_axis=1, tiled=True)
-    mixed = query * (long_conv.astype(jnp.float32) + skip_bias * gated)
-    squares = lax.psum(jnp.sum(mixed * mixed, axis=1), "ch")
-    scale = lax.rsqrt(squares / D + 1e-05)
-    normed = (mixed * scale[:, None] * norm_gain).astype(jnp.bfloat16)
-    return (mixed.astype(jnp.bfloat16), normed)
+    narrow, wide = jnp.bfloat16, jnp.float32
+    scratch = [pltpu.VMEM((rows, channels), narrow)] * 3 + [pltpu.VMEM((rows, channels), wide)]
+    scratch += [pltpu.VMEM(t.shape, narrow) for t in tables]
+    scratch += [pltpu.VMEM((3, 16, channels), narrow)]
+    scratch += [pltpu.VMEM((seq, LANES), narrow)] * 6
+    scratch += [pltpu.VMEM((seq, LANES), wide)] * 2
+    scratch += [pltpu.VMEM((rows, LANES), wide)] * 2
+    scratch += spectrum_scratch(inner)
+    scratch += [pltpu.SemaphoreType.DMA((8,))]
+    scratch += [pltpu.SemaphoreType.DMA((3,))] * 2
+    scratch += [pltpu.SemaphoreType.DMA((n,))] * 6
+    scratch += [pltpu.SemaphoreType.DMA((2,))]
+    whole = pl.BlockSpec(memory_space=pltpu.VMEM)
+    away = pl.BlockSpec(memory_space=pl.ANY)
+    out = jax.ShapeDtypeStruct((rows, channels), narrow)
+    return tuple(pl.pallas_call(
+        functools.partial(mixer_kernel, n, inner),
+        out_shape=(out, out),
+        in_specs=[away] * 8 + [whole] * 3,
+        out_specs=(whole, whole),
+        scratch_shapes=scratch,
+        compiler_params=pltpu.CompilerParams(
+            collective_id=0, has_side_effects=True, vmem_limit_bytes=48 * 2**20
+        ),
+    )(
+        q_proj, k_proj, v_proj, long_filter, *tables,
+        feat_filter.reshape(-1, 1, channels), skip_bias.reshape(1, -1), norm_gain.reshape(1, -1),
+    ))
 
 
 def solution(mesh):
     def layer(*arrays):
         rows, channels = arrays[0].shape
-        seq = rows * mesh.shape["seq"]
-        whole_lanes = channels == LANES * mesh.shape["seq"]
-        if whole_lanes and seq % (HALF * 256) == 0 and seq <= 2048:
+        n = mesh.shape["seq"]
+        seq = rows * n
+        whole_lanes = channels == LANES * n and n % 2 == 0 and mesh.shape["ch"] == 2
+        if whole_lanes and rows % 16 == 0 and seq % (2 * HALF * CHUNK) == 0 and seq <= 2048:
             return channel_shards(*arrays)
         return shards(*arrays)
 

time: 90.5 us -> 69.6 us (0.77)
  blocking collectives: 53 us -> 0 us
  Pallas kernels: 20.3 us -> 58.1 us
  local copies, waits for them, and re-layouts: 5.02 us -> 10.4 us
  other arithmetic: 4.88 us -> 0 us
  starting transfers between devices: 4.84 us -> 0 us
  waiting for transfers between devices: 1.3 us -> 0 us
    all_to_all x2 -> x0, blocking collectives: 50.5 us -> none  [the longest x1 32.9 us: channel_shards(): lax.all_to_all(signals, 'seq', split_axis=2, concat_axis=1, tiled=True)]
    pallas_call x1, Pallas kernels: 20.3 us -> 58.1 us  [channel_shards(): pl.pallas_call(functools.partial(mixer_kernel, n, inner), out_shape=(out,...]
    unnamed x24 -> x18, local copies, waits for them, and re-layouts: 1.6 us -> 9.41 us
    ppermute x1 -> x0, starting transfers between devices: 4.84 us -> none  [shifted(): return lax.ppermute(block, axis, route)]
    all_to_all x1 -> x0, local copies, waits for them, and re-layouts: 2.54 us -> none  [channel_shards(): lax.all_to_all(signals, 'seq', split_axis=2, concat_axis=1, tiled=True)]
    psum x1 -> x0, blocking collectives: 2.47 us -> none  [channel_shards(): squares = lax.psum(jnp.sum(mixed * mixed, axis=1), 'ch')]
    another operation x4 -> x0, other arithmetic: 1.95 us -> none  [the longest x1 1.68 us: channel_shards(): stacked = jnp.stack([q_proj, k_proj, v_proj])]
    ppermute x1 -> x0, waiting for transfers between devices: 1.3 us -> none  [shifted(): return lax.ppermute(block, axis, route)]
  transfers between devices with their start and end apart: 1 -> 0, of which waited for: 1 -> 0; matrix products, arithmetic and copies ran while one was open for 0% -> 0% of each run, Pallas kernels for 0% -> 0%
where the time goes in v2:
time: 69.6 us; the launch traced here: 69.1 us
  Pallas kernels  58.1 us (83%)
  local copies, waits for them, and re-layouts  10.4 us (15%)
    pallas_call x1, Pallas kernels, channel_shards(): pl.pallas_call(functools.partial(mixer_kernel, n, inner), out_shape=(out,...  58.1 us
    unnamed x18, local copies, waits for them, and re-layouts  9.41 us

profile of v2, /device:TPU:0, one launch (start us, length us, event | category | flops | bytes accessed | tf_op | source)
XLA Modules:
  0.0 69.1 jit_solution(9889887825733524857)
XLA Ops:
  0.6 1.0 %reshape.13.feat_ref = f32[9,1,2048]{2,1,0:T(1,128)S(1)} reshape(f32[3,3,2048]{2,1,0:T(4,128)} %param.14) | data formatting | bytes 147456 | tf_op jit(solution)/shard_map/reshape | solution.py:545
  1.6 0.0 copy-start
  1.6 1.2 %copy-done = f32[128,2048]{1,0:T(8,128)S(1)} copy-done((f32[128,2048]{1,0:T(8,128)S(1)}, f32[128,2048]{1,0:T(8,128)}, u32[]{:S(2)}) %copy-start) | copy-done | bytes 1048600
  2.9 0.0 copy-start.1
  2.9 1.0 %copy-done.1 = bf16[128,2048]{1,0:T(8,128)(2,1)S(1)} copy-done((bf16[128,2048]{1,0:T(8,128)(2,1)S(1)}, bf16[128,2048]{1,0:T(8,128)(2,1)}, u32[]{:S(2)}) %copy-start.1) | copy-done | bytes 524312
  3.9 0.0 copy-start.2
  3.9 1.0 %copy-done.2 = bf16[128,2048]{1,0:T(8,128)(2,1)S(1)} copy-done((bf16[128,2048]{1,0:T(8,128)(2,1)S(1)}, bf16[128,2048]{1,0:T(8,128)(2,1)}, u32[]{:S(2)}) %copy-start.2) | copy-done | bytes 524312
  4.9 0.0 copy-start.3
  4.9 1.0 %copy-done.3 = bf16[128,2048]{1,0:T(8,128)(2,1)S(1)} copy-done((bf16[128,2048]{1,0:T(8,128)(2,1)S(1)}, bf16[128,2048]{1,0:T(8,128)(2,1)}, u32[]{:S(2)}) %copy-start.3) | copy-done | bytes 524312
  6.0 0.0 copy-start.4
  6.0 1.0 %copy-done.4 = bf16[2,256,512]{2,1,0:T(8,128)(2,1)S(1)} copy-done((bf16[2,256,512]{2,1,0:T(8,128)(2,1)S(1)}, bf16[2,256,512]{2,1,0:T(8,128)(2,1)}, u32[]{:S(2)}) %copy-start.4) | copy-done | bytes 524312
  7.0 0.0 copy-start.5
  7.0 1.0 %copy-done.5 = bf16[2,256,512]{2,1,0:T(8,128)(2,1)S(1)} copy-done((bf16[2,256,512]{2,1,0:T(8,128)(2,1)S(1)}, bf16[2,256,512]{2,1,0:T(8,128)(2,1)}, u32[]{:S(2)}) %copy-start.5) | copy-done | bytes 524312
  8.1 0.0 copy-start.6
  8.1 0.7 %copy-done.6 = f32[2048]{0:T(1024)S(1)} copy-done((f32[2048]{0:T(1024)S(1)}, f32[2048]{0:T(1024)}, u32[]{:S(2)}) %copy-start.6) | copy-done | bytes 8216
  8.8 0.0 copy-start.7
  8.8 0.7 %copy-done.7 = f32[2048]{0:T(1024)S(1)} copy-done((f32[2048]{0:T(1024)S(1)}, f32[2048]{0:T(1024)}, u32[]{:S(2)}) %copy-start.7) | copy-done | bytes 8216
  9.5 58.1 %shard_map.122 = (bf16[128,2048]{1,0:T(8,128)(2,1)S(1)}, bf16[128,2048]{1,0:T(8,128)(2,1)S(1)}) custom-call(bf16[128,2048]{1,0:T(8,128)(2,1)S(1)} %copy-done.1, bf16[128,2048]{1,0:T(8,128)(2,1)S(1)} %copy-done.2, bf16[128,2048]{1,0:T(8,128)(2,1)S(1)} %copy-done.3, f32[128,2048]{1,0:T(8,128)S(1)} %copy-done, bf16[7,512,1024]{2,1,0:T(8,128)(2,1)} %constant.8.clone.f_full_hbm, ...), custom_call_target="tpu_custom_call" | custom-call | tf_op jit(solution)/shard_map/pallas_call | solution.py:534
  67.5 0.8 %copy.15 = bf16[128,2048]{1,0:T(8,128)(2,1)} copy(bf16[128,2048]{1,0:T(8,128)(2,1)S(1)} %get-tuple-element.4) | data formatting | bytes 1048576
  68.3 0.8 %copy.16 = bf16[128,2048]{1,0:T(8,128)(2,1)} copy(bf16[128,2048]{1,0:T(8,128)(2,1)S(1)} %get-tuple-element.5) | data formatting | bytes 1048576
Async XLA Ops:
  1.6 1.2 %copy-start = (f32[128,2048]{1,0:T(8,128)S(1)}, f32[128,2048]{1,0:T(8,128)}, u32[]{:S(2)}) copy-start(f32[128,2048]{1,0:T(8,128)} %filter_hbm.1) | copy-start | bytes 3145732
  2.9 1.0 %copy-start.1 = (bf16[128,2048]{1,0:T(8,128)(2,1)S(1)}, bf16[128,2048]{1,0:T(8,128)(2,1)}, u32[]{:S(2)}) copy-start(bf16[128,2048]{1,0:T(8,128)(2,1)} %q_hbm.1) | copy-start | bytes 1572868
  3.9 1.0 %copy-start.2 = (bf16[128,2048]{1,0:T(8,128)(2,1)S(1)}, bf16[128,2048]{1,0:T(8,128)(2,1)}, u32[]{:S(2)}) copy-start(bf16[128,2048]{1,0:T(8,128)(2,1)} %k_hbm.1) | copy-start | bytes 1572868
  4.9 1.0 %copy-start.3 = (bf16[128,2048]{1,0:T(8,128)(2,1)S(1)}, bf16[128,2048]{1,0:T(8,128)(2,1)}, u32[]{:S(2)}) copy-start(bf16[128,2048]{1,0:T(8,128)(2,1)} %v_hbm.1) | copy-start | bytes 1572868
  6.0 1.0 %copy-start.4 = (bf16[2,256,512]{2,1,0:T(8,128)(2,1)S(1)}, bf16[2,256,512]{2,1,0:T(8,128)(2,1)}, u32[]{:S(2)}) copy-start(bf16[2,256,512]{2,1,0:T(8,128)(2,1)} %constant.11.clone.g_real_hbm) | copy-start | bytes 1572868
  7.0 1.0 %copy-start.5 = (bf16[2,256,512]{2,1,0:T(8,128)(2,1)S(1)}, bf16[2,256,512]{2,1,0:T(8,128)(2,1)}, u32[]{:S(2)}) copy-start(bf16[2,256,512]{2,1,0:T(8,128)(2,1)} %constant.9.clone.f_real_hbm) | copy-start | bytes 1572868
  8.1 0.7 %copy-start.6 = (f32[2048]{0:T(1024)S(1)}, f32[2048]{0:T(1024)}, u32[]{:S(2)}) copy-start(f32[2048]{0:T(1024)} %param.16) | copy-start | bytes 24580
  8.8 0.7 %copy-start.7 = (f32[2048]{0:T(1024)S(1)}, f32[2048]{0:T(1024)}, u32[]{:S(2)}) copy-start(f32[2048]{0:T(1024)} %param.17) | copy-start | bytes 24580

commit v3 on v2

--- a/solution.py
+++ b/solution.py
@@ -13,6 +13,7 @@
 RADIX = 16
 HALF = RADIX // 2
 LANES = 128
+VMEM_BYTES = 62 * 2**20
 MESH = pl.DeviceIdType.MESH
 
 
@@ -44,7 +45,7 @@
 
     full, real = np.stack(full), np.stack(real)
     turn = lambda a: np.swapaxes(a, 1, 2)
-    return split(full), split(real), split(turn(full)), split(turn(real))
+    return split(full), split(real), turn(full).astype(jnp.bfloat16), turn(real).astype(jnp.bfloat16)
 
 
 def turned(cr, ci, a):
@@ -110,37 +111,49 @@
     return out
 
 
-CHUNK = 32
-
-
-def spread_blocks(inner, load, y_full, y_real):
+CHUNK = 16
+
+
+def spread_blocks(inner, load, y_full, y_real, rest=None):
+    def put(ref, low_ref, k, rows, value):
+        high = value.astype(jnp.bfloat16)
+        ref[k, rows, :] = high
+        if low_ref is not None:
+            low_ref[k, rows, :] = (value - high.astype(jnp.float32)).astype(jnp.bfloat16)
+
+    low_full, low_real = rest or (None, None)
+
     def step(i, carry):
         start = pl.multiple_of(i * CHUNK, CHUNK)
         rows = pl.ds(start, CHUNK)
         out = block_dft([load(n, start) for n in range(HALF)])
-        y_real[0, rows, :] = out[0].astype(jnp.bfloat16)
-        y_real[1, rows, :] = out[HALF].astype(jnp.bfloat16)
+        put(y_real, low_real, 0, rows, out[0])
+        put(y_real, low_real, 1, rows, out[HALF])
         lower = pl.ds(pl.multiple_of(inner + start, CHUNK), CHUNK)
         for k in range(1, HALF):
-            y_full[k - 1, rows, :] = out[k][0].astype(jnp.bfloat16)
-            y_full[k - 1, lower, :] = out[k][1].astype(jnp.bfloat16)
+            put(y_full, low_full, k - 1, rows, out[k][0])
+            put(y_full, low_full, k - 1, lower, out[k][1])
         return carry
 
     lax.fori_loop(0, inner // CHUNK, step, 0)
 
 
-def both(table, values):
+def dot(table, values):
+    return jnp.dot(table, values, preferred_element_type=jnp.float32)
+
+
+def careful(table, values, low):
     half = table.shape[1] // 2
-    first = jnp.dot(table[:, :half], values, preferred_element_type=jnp.float32)
-    return first + jnp.dot(table[:, half:], values, preferred_element_type=jnp.float32)
-
-
-def filter_spectrum(f_full, f_real, y_full, y_real, h_full, h_real):
+    first = dot(table[:, :half], values) + dot(table[:, half:], values)
+    return first + dot(table[:, :half], low)
+
+
+def filter_spectrum(f_full, f_real, y_full, y_real, low_full, low_real, h_full, h_real):
     for i in range(2):
-        h_real[i] = both(f_real[i], y_real[i])
+        h_real[i] = careful(f_real[i], y_real[i], low_real[i])
 
     def step(k, carry):
-        h_full[k] = both(f_full[k], y_full[k])
+        h_full[k] = careful(f_full[k], y_full[k], low_full[k])
         return carry
 
     lax.fori_loop(0, HALF - 1, step, 0)
@@ -155,7 +168,7 @@
 
     for i in range(2):
         half = inner // 2
-        a, b = both(f_real[i], y_real[i]), h_real[i]
+        a, b = dot(f_real[i, :, :inner], y_real[i]), h_real[i]
         pr, pi = product(a, b, half)
         pr, pi = pr * (2.0 / length), pi * (2.0 / length)
         if i == 0:
@@ -163,12 +176,12 @@
             pr = jnp.where(top, a[:half] * b[:half] * (1.0 / length), pr)
             pi = jnp.where(top, a[half:] * b[half:] * (1.0 / length), pi)
         z = jnp.concatenate([pr, pi]).astype(jnp.bfloat16)
-        h_real[i] = both(g_real[i], z)
+        h_real[i] = dot(g_real[i], z)
 
     def step(k, carry):
-        pr, pi = product(both(f_full[k], y_full[k]), h_full[k], inner)
+        pr, pi = product(dot(f_full[k, :, : 2 * inner], y_full[k]), h_full[k], inner)
         z = (jnp.concatenate([pr, pi]) * (2.0 / length)).astype(jnp.bfloat16)
-        h_full[k] = both(g_full[k], z)
+        h_full[k] = dot(g_full[k], z)
         return carry
 
     lax.fori_loop(0, HALF - 1, step, 0)
@@ -192,6 +205,8 @@
 def spectrum_scratch(inner):
     wide = (HALF - 1, 2 * inner, LANES)
     return [
+        pltpu.VMEM(wide, jnp.bfloat16),
+        pltpu.VMEM((2, inner, LANES), jnp.bfloat16),
         pltpu.VMEM(wide, jnp.bfloat16),
         pltpu.VMEM((2, inner, LANES), jnp.bfloat16),
         pltpu.VMEM(wide, jnp.float32),
@@ -307,12 +322,12 @@
 def mixer_kernel(
     n, inner,
     q_hbm, k_hbm, v_hbm, filter_hbm, f_full_hbm, f_real_hbm, g_full_hbm, g_real_hbm,
-    feat_ref, skip_ref, gain_ref,
-    mixed_ref, normed_ref,
-    q_ref, k_ref, v_ref, filter_ref, f_full, f_real, g_full, g_real,
+    feat_hbm, skip_hbm,
+    mixed_hbm, scale_ref,
+    feat_ref, skip_ref, q_ref, k_ref, v_ref, filter_ref, f_full, f_real, g_full, g_real,
     tails, send_f, send_g, send_y, recv_f, recv_g, recv_y, query, gated, sums, other_sums,
-    y_full, y_real, h_full, h_real,
-    local_sem, tail_send, tail_recv, f_send, f_recv, g_send, g_recv, y_send, y_recv, sum_sem,
+    y_full, y_real, low_full, low_real, h_full, h_real,
+    local_sem, tail_send, tail_recv, f_send, f_recv, g_send, g_recv, y_send, y_recv, sum_sem, out_sem,
 ):
     me = lax.axis_index("seq")
     core = lax.axis_index("ch")
@@ -334,10 +349,11 @@
         pltpu.make_async_copy(source, target, local_sem.at[i])
         for i, (source, target) in enumerate([
             (filter_hbm, filter_ref), (k_hbm, k_ref), (v_hbm, v_ref), (q_hbm, q_ref),
+            (feat_hbm, feat_ref), (skip_hbm, skip_ref),
             (f_real_hbm, f_real), (f_full_hbm, f_full), (g_real_hbm, g_real), (g_full_hbm, g_full),
         ])
     ]
-    for load in loads:
+    for load in loads[:6]:
         load.start()
 
     barrier = pltpu.get_barrier_semaphore()
@@ -359,7 +375,7 @@
 
     lax.fori_loop(0, n, narrow, 0)
     recv_f[at(me), :] = send_f[at(me), :]
-    for load in loads[1:4]:
+    for load in loads[1:6]:
         load.wait()
     pl.semaphore_wait(barrier, n)
 
@@ -414,12 +430,15 @@
             lambda: lax.fori_loop(0, n - 1, start, 0),
             lambda: lax.fori_loop(0, n - 1, arrive, 0),
             lambda: lax.fori_loop(0, n - 1, leave, 0),
+            come,
         )
 
-    start_f, arrive_f, leave_f = exchange(send_f, recv_f, f_send, f_recv)
-    start_g, arrive_g, leave_g = exchange(send_g, recv_g, g_send, g_recv)
-    start_y, arrive_y, leave_y = exchange(send_y, recv_y, y_send, y_recv)
+    start_f, arrive_f, leave_f, _ = exchange(send_f, recv_f, f_send, f_recv)
+    start_g, arrive_g, leave_g, _ = exchange(send_g, recv_g, g_send, g_recv)
+    start_y, _, leave_y, come_y = exchange(send_y, recv_y, y_send, y_recv)
     start_f()
+    for load in loads[6:]:
+        load.start()
 
     first = me == 0
 
@@ -428,10 +447,10 @@
         before = tails[tail, :, columns].astype(jnp.float32)
         before = jnp.where(first, 0.0, before)
         window = jnp.concatenate([before, ref[:, columns].astype(jnp.float32)])
-        total = feat_ref[3 * stream, :, columns] * window[16:]
+        total = feat_ref[stream, 0:1, columns] * window[16:]
         for tap in (1, 2):
             moved = pltpu.roll(window, tap, 0)[16:]
-            total = total + feat_ref[3 * stream + tap, :, columns] * moved
+            total = total + feat_ref[stream, tap : tap + 1, columns] * moved
         return total
 
     for copy in tail_copies[:2]:
@@ -464,30 +483,36 @@
     def store(block, start, value):
         send_y[pl.ds(pl.multiple_of(block * inner + start, CHUNK), CHUNK), :] = value
 
-    for load in loads[4:]:
+    for load in loads[6:]:
         load.wait()
     arrive_f()
-    spread_blocks(inner, block_of(recv_f), y_full, y_real)
-    filter_spectrum(f_full, f_real, y_full, y_real, h_full, h_real)
+    spread_blocks(inner, block_of(recv_f), y_full, y_real, (low_full, low_real))
+    filter_spectrum(f_full, f_real, y_full, y_real, low_full, low_real, h_full, h_real)
     arrive_g()
     spread_blocks(inner, block_of(recv_g), y_full, y_real)
     filtered(inner, f_full, f_real, g_full, g_real, y_full, y_real, h_full, h_real)
     gather_blocks(inner, h_full, h_real, store)
     start_y()
     recv_y[at(me), :] = send_y[at(me), :]
-    leave_f()
-    leave_g()
-    arrive_y()
-
-    def mix(j, carry):
-        conv = recv_y[at(j), :].astype(jnp.float32)
-        mixed = query[at(j), :] * (conv + skip_ref[:, lanes(j)] * gated[at(j), :])
-        query[at(j), :] = mixed
-        mixed_ref[:, lanes(j)] = mixed.astype(jnp.bfloat16)
-        return carry + mixed * mixed
-
-    squares = lax.fori_loop(0, n, mix, jnp.zeros((rows, LANES), jnp.float32))
-    sums[...] = squares
+
+    def out_copy(block):
+        return pltpu.make_async_copy(
+            query.at[at(block), :], mixed_hbm.at[:, lanes(block)], out_sem.at[block]
+        )
+
+    def mix(block):
+        conv = recv_y[at(block), :].astype(jnp.float32)
+        mixed = query[at(block), :] * (conv + skip_ref[:, lanes(block)] * gated[at(block), :])
+        query[at(block), :] = mixed
+        out_copy(block).start()
+        return mixed * mixed
+
+    def mix_next(j, carry):
+        block = partner(n - 2 - j)
+        come_y(block).wait_recv()
+        return carry + mix(block)
+
+    sums[...] = lax.fori_loop(0, n - 1, mix_next, mix(me))
     sum_copy = pltpu.make_async_remote_copy(
         src_ref=sums,
         dst_ref=other_sums,
@@ -497,17 +522,18 @@
         device_id_type=MESH,
     )
     sum_copy.start()
+    leave_f()
+    leave_g()
     leave_y()
+
+    def written(j, carry):
+        out_copy(j).wait()
+        return carry
+
+    lax.fori_loop(0, n, written, 0)
     sum_copy.wait()
     total = jnp.sum(sums[...] + other_sums[...], axis=1, keepdims=True)
-    scale = lax.rsqrt(total / D + 1e-05)
-
-    def norm(j, carry):
-        value = query[at(j), :] * scale * gain_ref[:, lanes(j)]
-        normed_ref[:, lanes(j)] = value.astype(jnp.bfloat16)
-        return carry
-
-    lax.fori_loop(0, n, norm, 0)
+    scale_ref[...] = jnp.broadcast_to(lax.rsqrt(total / D + 1e-05), scale_ref.shape)
 
 
 def channel_shards(q_proj, k_proj, v_proj, feat_filter, long_filter, skip_bias, norm_gain):
@@ -517,33 +543,36 @@
     inner = seq // HALF
     tables = [jnp.asarray(t) for t in dft_tables(seq)]
     narrow, wide = jnp.bfloat16, jnp.float32
-    scratch = [pltpu.VMEM((rows, channels), narrow)] * 3 + [pltpu.VMEM((rows, channels), wide)]
+    scratch = [pltpu.VMEM(feat_filter.shape, wide), pltpu.VMEM((1, channels), wide)]
+    scratch += [pltpu.VMEM((rows, channels), narrow)] * 3 + [pltpu.VMEM((rows, channels), wide)]
     scratch += [pltpu.VMEM(t.shape, narrow) for t in tables]
     scratch += [pltpu.VMEM((3, 16, channels), narrow)]
     scratch += [pltpu.VMEM((seq, LANES), narrow)] * 6
     scratch += [pltpu.VMEM((seq, LANES), wide)] * 2
     scratch += [pltpu.VMEM((rows, LANES), wide)] * 2
     scratch += spectrum_scratch(inner)
-    scratch += [pltpu.SemaphoreType.DMA((8,))]
+    scratch += [pltpu.SemaphoreType.DMA((10,))]
     scratch += [pltpu.SemaphoreType.DMA((3,))] * 2
     scratch += [pltpu.SemaphoreType.DMA((n,))] * 6
-    scratch += [pltpu.SemaphoreType.DMA((2,))]
-    whole = pl.BlockSpec(memory_space=pltpu.VMEM)
+    scratch += [pltpu.SemaphoreType.DMA((2,)), pltpu.SemaphoreType.DMA((n,))]
     away = pl.BlockSpec(memory_space=pl.ANY)
-    out = jax.ShapeDtypeStruct((rows, channels), narrow)
-    return tuple(pl.pallas_call(
+    mixed, scale = pl.pallas_call(
         functools.partial(mixer_kernel, n, inner),
-        out_shape=(out, out),
-        in_specs=[away] * 8 + [whole] * 3,
-        out_specs=(whole, whole),
+        out_shape=(
+            jax.ShapeDtypeStruct((rows, channels), wide),
+            jax.ShapeDtypeStruct((rows, LANES), wide),
+        ),
+        in_specs=[away] * 10,
+        out_specs=(away, pl.BlockSpec(memory_space=pltpu.VMEM)),
         scratch_shapes=scratch,
         compiler_params=pltpu.CompilerParams(
-            collective_id=0, has_side_effects=True, vmem_limit_bytes=48 * 2**20
+            collective_id=0, has_side_effects=True, vmem_limit_bytes=VMEM_BYTES
         ),
     )(
-        q_proj, k_proj, v_proj, long_filter, *tables,
-        feat_filter.reshape(-1, 1, channels), skip_bias.reshape(1, -1), norm_gain.reshape(1, -1),
-    ))
+        q_proj, k_proj, v_proj, long_filter, *tables, feat_filter, skip_bias.reshape(1, -1)
+    )
+    normed = mixed * scale[:, :1] * norm_gain
+    return (mixed.astype(narrow), normed.astype(narrow))
 
 
 def solution(mesh):

time: 69.6 us -> 58.9 us (0.85)
  local copies, waits for them, and re-layouts: 10.4 us -> 0.95 us
  Pallas kernels: 58.1 us -> 54.4 us
  other arithmetic: 0 us -> 2.67 us
    unnamed x18 -> x2, local copies, waits for them, and re-layouts: 9.41 us -> 0.01 us
    pallas_call x1, Pallas kernels: 58.1 us -> 54.4 us  [channel_shards(): pl.pallas_call(functools.partial(mixer_kernel, n, inner), out_shape=(jax....]
    convert_element_type x0 -> x1, other arithmetic: none -> 2.67 us  [channel_shards(): return (mixed.astype(narrow), normed.astype(narrow))]
    reshape x1 -> x0, local copies, waits for them, and re-layouts: 1 us -> none  [channel_shards(): feat_filter.reshape(-1, 1, channels)]
    slice x0 -> x1, local copies, waits for them, and re-layouts: none -> 0.94 us  [channel_shards(): normed = mixed * scale[:, :1] * norm_gain]
where the time goes in v3:
time: 58.9 us; the launch traced here: 58.7 us
  Pallas kernels  54.4 us (92%)
  other arithmetic  2.67 us (5%)
  local copies, waits for them, and re-layouts  0.95 us (2%)
  between operations  0.66 us (1%)
    pallas_call x1, Pallas kernels, channel_shards(): pl.pallas_call(functools.partial(mixer_kernel, n, inner), out_shape=(jax....  54.4 us
    convert_element_type x1, other arithmetic, channel_shards(): return (mixed.astype(narrow), normed.astype(narrow))  2.67 us

profile of v3, /device:TPU:0, one launch (start us, length us, event | category | flops | bytes accessed | tf_op | source)
XLA Modules:
  0.0 58.7 jit_solution(7610054682843716193)
XLA Ops:
  0.6 0.0 copy-start
  0.6 54.4 %shard_map.122 = (f32[128,2048]{1,0:T(8,128)}, f32[128,128]{1,0:T(8,128)}) custom-call(bf16[128,2048]{1,0:T(8,128)(2,1)} %q_hbm.1, bf16[128,2048]{1,0:T(8,128)(2,1)} %k_hbm.1, bf16[128,2048]{1,0:T(8,128)(2,1)} %v_hbm.1, f32[128,2048]{1,0:T(8,128)} %filter_hbm.1, bf16[7,512,1024]{2,1,0:T(8,128)(2,1)} %constant.8.clone.f_full_hbm, ...), custom_call_target="tpu_custom_call" | custom-call | tf_op jit(solution)/shard_map/pallas_call | solution.py:559
  55.1 0.9 %slice_reduce_fusion = f32[128]{0:T(128)S(1)} fusion(f32[128,128]{1,0:T(8,128)} %get-tuple-element.5), kind=kLoop, calls=%fused_computation.1 | loop fusion | bytes 1024 | tf_op jit(solution)/shard_map/slice | solution.py:574
  56.0 0.0 copy-done
  56.1 2.7 %multiply_convert_fusion = (bf16[128,2048]{1,0:T(8,128)(2,1)}, bf16[128,2048]{1,0:T(8,128)(2,1)}) fusion(f32[128,2048]{1,0:T(8,128)} %get-tuple-element.4, f32[2048]{0:T(1024)S(1)} %copy-done, f32[128]{0:T(128)S(1)} %slice_reduce_fusion), kind=kLoop, calls=%fused_computation | loop fusion | flops 1048576 | bytes 2105856 | tf_op jit(solution)/shard_map/convert_element_type | solution.py:575
Async XLA Ops:
  0.6 55.4 %copy-start = (f32[2048]{0:T(1024)S(1)}, f32[2048]{0:T(1024)}, u32[]{:S(2)}) copy-start(f32[2048]{0:T(1024)} %param.17) | copy-start | bytes 24580

commit v4 on v3

--- a/solution.py
+++ b/solution.py
@@ -322,9 +322,9 @@
 def mixer_kernel(
     n, inner,
     q_hbm, k_hbm, v_hbm, filter_hbm, f_full_hbm, f_real_hbm, g_full_hbm, g_real_hbm,
-    feat_hbm, skip_hbm,
-    mixed_hbm, scale_ref,
-    feat_ref, skip_ref, q_ref, k_ref, v_ref, filter_ref, f_full, f_real, g_full, g_real,
+    feat_hbm, skip_hbm, gain_hbm,
+    mixed_hbm, normed_hbm,
+    feat_ref, skip_ref, gain_ref, mixed_ref, normed_ref, q_ref, k_ref, v_ref, filter_ref, f_full, f_real, g_full, g_real,
     tails, send_f, send_g, send_y, recv_f, recv_g, recv_y, query, gated, sums, other_sums,
     y_full, y_real, low_full, low_real, h_full, h_real,
     local_sem, tail_send, tail_recv, f_send, f_recv, g_send, g_recv, y_send, y_recv, sum_sem, out_sem,
@@ -342,18 +342,19 @@
         return pl.ds(pl.multiple_of(block * LANES, LANES), LANES)
 
     def partner(j):
-        offset = n // 2 + ((j + 1) // 2) * (2 * (j % 2) - 1)
+        quarter = n // 4
+        offset = (3 - j % 4) * quarter + quarter - 1 - j // 4
         return lax.rem(me + offset, n)
 
     loads = [
         pltpu.make_async_copy(source, target, local_sem.at[i])
         for i, (source, target) in enumerate([
             (filter_hbm, filter_ref), (k_hbm, k_ref), (v_hbm, v_ref), (q_hbm, q_ref),
-            (feat_hbm, feat_ref), (skip_hbm, skip_ref),
+            (feat_hbm, feat_ref), (skip_hbm, skip_ref), (gain_hbm, gain_ref),
             (f_real_hbm, f_real), (f_full_hbm, f_full), (g_real_hbm, g_real), (g_full_hbm, g_full),
         ])
     ]
-    for load in loads[:6]:
+    for load in loads[:7]:
         load.start()
 
     barrier = pltpu.get_barrier_semaphore()
@@ -375,7 +376,7 @@
 
     lax.fori_loop(0, n, narrow, 0)
     recv_f[at(me), :] = send_f[at(me), :]
-    for load in loads[1:6]:
+    for load in loads[1:7]:
         load.wait()
     pl.semaphore_wait(barrier, n)
 
@@ -437,7 +438,7 @@
     start_g, arrive_g, leave_g, _ = exchange(send_g, recv_g, g_send, g_recv)
     start_y, _, leave_y, come_y = exchange(send_y, recv_y, y_send, y_recv)
     start_f()
-    for load in loads[6:]:
+    for load in loads[7:]:
         load.start()
 
     first = me == 0
@@ -483,7 +484,7 @@
     def store(block, start, value):
         send_y[pl.ds(pl.multiple_of(block * inner + start, CHUNK), CHUNK), :] = value
 
-    for load in loads[6:]:
+    for load in loads[7:]:
         load.wait()
     arrive_f()
     spread_blocks(inner, block_of(recv_f), y_full, y_real, (low_full, low_real))
@@ -495,16 +496,14 @@
     start_y()
     recv_y[at(me), :] = send_y[at(me), :]
 
-    def out_copy(block):
-        return pltpu.make_async_copy(
-            query.at[at(block), :], mixed_hbm.at[:, lanes(block)], out_sem.at[block]
-        )
+    mixed_copy = pltpu.make_async_copy(mixed_ref, mixed_hbm, out_sem.at[0])
+    normed_copy = pltpu.make_async_copy(normed_ref, normed_hbm, out_sem.at[1])
 
     def mix(block):
         conv = recv_y[at(block), :].astype(jnp.float32)
         mixed = query[at(block), :] * (conv + skip_ref[:, lanes(block)] * gated[at(block), :])
         query[at(block), :] = mixed
-        out_copy(block).start()
+        mixed_ref[:, lanes(block)] = mixed.astype(jnp.bfloat16)
         return mixed * mixed
 
     def mix_next(j, carry):
@@ -522,18 +521,23 @@
         device_id_type=MESH,
     )
     sum_copy.start()
+    mixed_copy.start()
     leave_f()
     leave_g()
     leave_y()
-
-    def written(j, carry):
-        out_copy(j).wait()
-        return carry
-
-    lax.fori_loop(0, n, written, 0)
     sum_copy.wait()
     total = jnp.sum(sums[...] + other_sums[...], axis=1, keepdims=True)
-    scale_ref[...] = jnp.broadcast_to(lax.rsqrt(total / D + 1e-05), scale_ref.shape)
+    scale = lax.rsqrt(total / D + 1e-05)
+
+    def norm(j, carry):
+        value = query[at(j), :] * scale * gain_ref[:, lanes(j)]
+        normed_ref[:, lanes(j)] = value.astype(jnp.bfloat16)
+        return carry
+
+    lax.fori_loop(0, n, norm, 0)
+    normed_copy.start()
+    mixed_copy.wait()
+    normed_copy.wait()
 
 
 def channel_shards(q_proj, k_proj, v_proj, feat_filter, long_filter, skip_bias, norm_gain):
@@ -544,6 +548,7 @@
     tables = [jnp.asarray(t) for t in dft_tables(seq)]
     narrow, wide = jnp.bfloat16, jnp.float32
     scratch = [pltpu.VMEM(feat_filter.shape, wide), pltpu.VMEM((1, channels), wide)]
+    scratch += [pltpu.VMEM((1, channels), wide)] + [pltpu.VMEM((rows, channels), narrow)] * 2
     scratch += [pltpu.VMEM((rows, channels), narrow)] * 3 + [pltpu.VMEM((rows, channels), wide)]
     scratch += [pltpu.VMEM(t.shape, narrow) for t in tables]
     scratch += [pltpu.VMEM((3, 16, channels), narrow)]
@@ -551,28 +556,25 @@
     scratch += [pltpu.VMEM((seq, LANES), wide)] * 2
     scratch += [pltpu.VMEM((rows, LANES), wide)] * 2
     scratch += spectrum_scratch(inner)
-    scratch += [pltpu.SemaphoreType.DMA((10,))]
+    scratch += [pltpu.SemaphoreType.DMA((11,))]
     scratch += [pltpu.SemaphoreType.DMA((3,))] * 2
     scratch += [pltpu.SemaphoreType.DMA((n,))] * 6
-    scratch += [pltpu.SemaphoreType.DMA((2,)), pltpu.SemaphoreType.DMA((n,))]
+    scratch += [pltpu.SemaphoreType.DMA((2,))] * 2
     away = pl.BlockSpec(memory_space=pl.ANY)
-    mixed, scale = pl.pallas_call(
+    out = jax.ShapeDtypeStruct((rows, channels), narrow)
+    return tuple(pl.pallas_call(
         functools.partial(mixer_kernel, n, inner),
-        out_shape=(
-            jax.ShapeDtypeStruct((rows, channels), wide),
-            jax.ShapeDtypeStruct((rows, LANES), wide),
-        ),
-        in_specs=[away] * 10,
-        out_specs=(away, pl.BlockSpec(memory_space=pltpu.VMEM)),
+        out_shape=(out, out),
+        in_specs=[away] * 11,
+        out_specs=(away, away),
         scratch_shapes=scratch,
         compiler_params=pltpu.CompilerParams(
             collective_id=0, has_side_effects=True, vmem_limit_bytes=VMEM_BYTES
         ),
     )(
-        q_proj, k_proj, v_proj, long_filter, *tables, feat_filter, skip_bias.reshape(1, -1)
-    )
-    normed = mixed * scale[:, :1] * norm_gain
-    return (mixed.astype(narrow), normed.astype(narrow))
+        q_proj, k_proj, v_proj, long_filter, *tables,
+        feat_filter, skip_bias.reshape(1, -1), norm_gain.reshape(1, -1),
+    ))
 
 
 def solution(mesh):
@@ -580,7 +582,7 @@
         rows, channels = arrays[0].shape
         n = mesh.shape["seq"]
         seq = rows * n
-        whole_lanes = channels == LANES * n and n % 2 == 0 and mesh.shape["ch"] == 2
+        whole_lanes = channels == LANES * n and n % 4 == 0 and mesh.shape["ch"] == 2
         if whole_lanes and rows % 16 == 0 and seq % (2 * HALF * CHUNK) == 0 and seq <= 2048:
             return channel_shards(*arrays)
         return shards(*arrays)

time: 58.9 us -> 61.8 us (1.049)
  local copies, waits for them, and re-layouts: 0.95 us -> 3.76 us
  Pallas kernels: 54.4 us -> 57.2 us
  other arithmetic: 2.67 us -> 0 us
    unnamed x2, local copies, waits for them, and re-layouts: 0.01 us -> 3.76 us
    pallas_call x1, Pallas kernels: 54.4 us -> 57.2 us  [channel_shards(): pl.pallas_call(functools.partial(mixer_kernel, n, inner), out_shape=(out,...]
    convert_element_type x1 -> x0, other arithmetic: 2.67 us -> none  [channel_shards(): return (mixed.astype(narrow), normed.astype(narrow))]
    slice x1 -> x0, local copies, waits for them, and re-layouts: 0.94 us -> none  [channel_shards(): normed = mixed * scale[:, :1] * norm_gain]
where the time goes in v4:
time: 61.8 us; the launch traced here: 61.6 us
  Pallas kernels  57.2 us (93%)
  local copies, waits for them, and re-layouts  3.76 us (6%)
  between operations  0.64 us (1%)
    pallas_call x1, Pallas kernels, channel_shards(): pl.pallas_call(functools.partial(mixer_kernel, n, inner), out_shape=(out,...  57.2 us
    unnamed x2, local copies, waits for them, and re-layouts  3.76 us

profile of v4, /device:TPU:0, one launch (start us, length us, event | category | flops | bytes accessed | tf_op | source)
XLA Modules:
  0.0 61.6 jit_solution(14260839934591052489)
XLA Ops:
  0.6 57.2 %shard_map.122 = (bf16[128,2048]{1,0:T(8,128)(2,1)}, bf16[128,2048]{1,0:T(8,128)(2,1)}) custom-call(bf16[128,2048]{1,0:T(8,128)(2,1)} %q_hbm.1, bf16[128,2048]{1,0:T(8,128)(2,1)} %k_hbm.1, bf16[128,2048]{1,0:T(8,128)(2,1)} %v_hbm.1, f32[128,2048]{1,0:T(8,128)} %filter_hbm.1, bf16[7,512,1024]{2,1,0:T(8,128)(2,1)} %constant.8.clone.f_full_hbm, ...), custom_call_target="tpu_custom_call" | custom-call | tf_op jit(solution)/shard_map/pallas_call | solution.py:565
  57.8 1.9 %copy.15 = bf16[128,2048]{1,0:T(8,128)(2,1)} copy(bf16[128,2048]{1,0:T(8,128)(2,1)} %get-tuple-element.4) | data formatting | bytes 1048576
  59.7 1.9 %copy.16 = bf16[128,2048]{1,0:T(8,128)(2,1)} copy(bf16[128,2048]{1,0:T(8,128)(2,1)} %get-tuple-element.5) | data formatting | bytes 1048576

commit v5 on v4

--- a/solution.py
+++ b/solution.py
@@ -13,7 +13,7 @@
 RADIX = 16
 HALF = RADIX // 2
 LANES = 128
-VMEM_BYTES = 62 * 2**20
+VMEM_BYTES = 48 * 2**20
 MESH = pl.DeviceIdType.MESH
 
 
@@ -114,7 +114,7 @@
 CHUNK = 16
 
 
-def spread_blocks(inner, load, y_full, y_real, rest=None):
+def spread_blocks(inner, part, load, y_full, y_real, rest=None):
     def put(ref, low_ref, k, rows, value):
         high = value.astype(jnp.bfloat16)
         ref[k, rows, :] = high
@@ -123,10 +123,11 @@
 
     low_full, low_real = rest or (None, None)
 
-    def step(i, carry):
-        start = pl.multiple_of(i * CHUNK, CHUNK)
+    def step(first, i, carry):
+        offset = pl.multiple_of(i * CHUNK, CHUNK)
+        start = pl.multiple_of(first + offset, CHUNK)
         rows = pl.ds(start, CHUNK)
-        out = block_dft([load(n, start) for n in range(HALF)])
+        out = block_dft([load(n, first, offset) for n in range(HALF)])
         put(y_real, low_real, 0, rows, out[0])
         put(y_real, low_real, 1, rows, out[HALF])
         lower = pl.ds(pl.multiple_of(inner + start, CHUNK), CHUNK)
@@ -135,7 +136,8 @@
             put(y_full, low_full, k - 1, lower, out[k][1])
         return carry
 
-    lax.fori_loop(0, inner // CHUNK, step, 0)
+    for first in range(0, inner, part):
+        lax.fori_loop(0, part // CHUNK, functools.partial(step, first), 0)
 
 
 def dot(table, values):
@@ -159,7 +161,7 @@
     lax.fori_loop(0, HALF - 1, step, 0)
 
 
-def filtered(inner, f_full, f_real, g_full, g_real, y_full, y_real, h_full, h_real):
+def filtered(inner, f_full, f_real, g_full, g_real, y_full, y_real, h_full, h_real, z_full, z_real):
     length = inner * RADIX
 
     def product(a, b, size):
@@ -176,30 +178,32 @@
             pr = jnp.where(top, a[:half] * b[:half] * (1.0 / length), pr)
             pi = jnp.where(top, a[half:] * b[half:] * (1.0 / length), pi)
         z = jnp.concatenate([pr, pi]).astype(jnp.bfloat16)
-        h_real[i] = dot(g_real[i], z)
+        z_real[i] = dot(g_real[i], z)
 
     def step(k, carry):
         pr, pi = product(dot(f_full[k, :, : 2 * inner], y_full[k]), h_full[k], inner)
         z = (jnp.concatenate([pr, pi]) * (2.0 / length)).astype(jnp.bfloat16)
-        h_full[k] = dot(g_full[k], z)
+        z_full[k] = dot(g_full[k], z)
         return carry
 
     lax.fori_loop(0, HALF - 1, step, 0)
 
 
-def gather_blocks(inner, h_full, h_real, store):
-    def step(i, carry):
-        start = pl.multiple_of(i * CHUNK, CHUNK)
+def gather_blocks(inner, part, h_full, h_real, store):
+    def step(first, i, carry):
+        offset = pl.multiple_of(i * CHUNK, CHUNK)
+        start = pl.multiple_of(first + offset, CHUNK)
         rows = pl.ds(start, CHUNK)
         lower = pl.ds(pl.multiple_of(inner + start, CHUNK), CHUNK)
         u = {0: h_real[0, rows, :], HALF: h_real[1, rows, :]}
         for k in range(1, HALF):
             u[k] = (h_full[k - 1, rows, :], h_full[k - 1, lower, :])
         for n, block in enumerate(block_idft(u)):
-            store(n, start, block.astype(jnp.bfloat16))
-        return carry
-
-    lax.fori_loop(0, inner // CHUNK, step, 0)
+            store(n, first, offset, block)
+        return carry
+
+    for first in range(0, inner, part):
+        lax.fori_loop(0, part // CHUNK, functools.partial(step, first), 0)
 
 
 def spectrum_scratch(inner):
@@ -209,6 +213,8 @@
         pltpu.VMEM((2, inner, LANES), jnp.bfloat16),
         pltpu.VMEM(wide, jnp.bfloat16),
         pltpu.VMEM((2, inner, LANES), jnp.bfloat16),
+        pltpu.VMEM(wide, jnp.float32),
+        pltpu.VMEM((2, inner, LANES), jnp.float32),
         pltpu.VMEM(wide, jnp.float32),
         pltpu.VMEM((2, inner, LANES), jnp.float32),
     ]
@@ -323,11 +329,13 @@
     n, inner,
     q_hbm, k_hbm, v_hbm, filter_hbm, f_full_hbm, f_real_hbm, g_full_hbm, g_real_hbm,
     feat_hbm, skip_hbm, gain_hbm,
-    mixed_hbm, normed_hbm,
-    feat_ref, skip_ref, gain_ref, mixed_ref, normed_ref, q_ref, k_ref, v_ref, filter_ref, f_full, f_real, g_full, g_real,
-    tails, send_f, send_g, send_y, recv_f, recv_g, recv_y, query, gated, sums, other_sums,
-    y_full, y_real, low_full, low_real, h_full, h_real,
-    local_sem, tail_send, tail_recv, f_send, f_recv, g_send, g_recv, y_send, y_recv, sum_sem, out_sem,
+    mixed_ref, normed_ref,
+    feat_ref, skip_ref, gain_ref, q_ref, k_ref, v_ref, filter_ref, f_full, f_real, g_full, g_real,
+    tails, send_f, recv_f, send_a, send_b, recv_a, recv_b,
+    send_ya, send_yb, recv_ya, recv_yb, query, gated, sums, other_sums,
+    y_full, y_real, low_full, low_real, h_full, h_real, z_full, z_real,
+    local_sem, tail_send, tail_recv, f_send, f_recv, a_send, a_recv, b_send, b_recv,
+    ya_send, ya_recv, yb_send, yb_recv, sum_sem,
 ):
     me = lax.axis_index("seq")
     core = lax.axis_index("ch")
@@ -338,12 +346,21 @@
     def at(block):
         return pl.ds(pl.multiple_of(block * rows, rows), rows)
 
+    part = rows // 2
+
+    def packed_at(block):
+        return pl.ds(pl.multiple_of(block * part, part), part)
+
+    def swap(value):
+        return pltpu.roll(value, LANES // 2, 1)
+
+    lower = lax.broadcasted_iota(jnp.int32, (part, LANES), 1) < LANES // 2
+
     def lanes(block):
         return pl.ds(pl.multiple_of(block * LANES, LANES), LANES)
 
     def partner(j):
-        quarter = n // 4
-        offset = (3 - j % 4) * quarter + quarter - 1 - j // 4
+        offset = n // 2 + ((j + 1) // 2) * (2 * (j % 2) - 1)
         return lax.rem(me + offset, n)
 
     loads = [
@@ -394,7 +411,7 @@
     for copy in tail_copies:
         copy.start()
 
-    def exchange(source, target, send_sem, recv_sem):
+    def exchange(at, source, target, send_sem, recv_sem):
         def to(peer):
             return pltpu.make_async_remote_copy(
                 src_ref=source.at[at(peer), :],
@@ -434,9 +451,11 @@
             come,
         )
 
-    start_f, arrive_f, leave_f, _ = exchange(send_f, recv_f, f_send, f_recv)
-    start_g, arrive_g, leave_g, _ = exchange(send_g, recv_g, g_send, g_recv)
-    start_y, _, leave_y, come_y = exchange(send_y, recv_y, y_send, y_recv)
+    start_f, arrive_f, leave_f, _ = exchange(at, send_f, recv_f, f_send, f_recv)
+    start_a, arrive_a, leave_a, _ = exchange(packed_at, send_a, recv_a, a_send, a_recv)
+    start_b, arrive_b, leave_b, _ = exchange(packed_at, send_b, recv_b, b_send, b_recv)
+    start_ya, _, leave_ya, come_ya = exchange(packed_at, send_ya, recv_ya, ya_send, ya_recv)
+    start_yb, _, leave_yb, come_yb = exchange(packed_at, send_yb, recv_yb, yb_send, yb_recv)
     start_f()
     for load in loads[7:]:
         load.start()
@@ -460,12 +479,18 @@
     def gate(j, carry):
         value = featured(1, 0, k_ref, j) * featured(2, 1, v_ref, j)
         gated[at(j), :] = value
-        send_g[at(j), :] = value.astype(jnp.bfloat16)
+        top, bottom = value[:part], value[part:]
+        half_a = jnp.where(lower, top, swap(bottom))
+        half_b = jnp.where(lower, swap(top), bottom)
+        send_a[packed_at(j), :] = half_a.astype(jnp.bfloat16)
+        send_b[packed_at(j), :] = half_b.astype(jnp.bfloat16)
         return carry
 
     lax.fori_loop(0, n, gate, 0)
-    start_g()
-    recv_g[at(me), :] = send_g[at(me), :]
+    start_a()
+    start_b()
+    recv_a[packed_at(me), :] = send_a[packed_at(me), :]
+    recv_b[packed_at(me), :] = send_b[packed_at(me), :]
     tail_copies[2].wait()
 
     def ask(j, carry):
@@ -474,33 +499,56 @@
 
     lax.fori_loop(0, n, ask, 0)
 
-    def block_of(ref):
-        def load(block, start):
-            where = pl.ds(pl.multiple_of(block * inner + start, CHUNK), CHUNK)
-            return ref[where, :].astype(jnp.float32)
-
-        return load
-
-    def store(block, start, value):
-        send_y[pl.ds(pl.multiple_of(block * inner + start, CHUNK), CHUNK), :] = value
+    def load_filter(block, first, offset):
+        where = pl.ds(pl.multiple_of(block * inner + first + offset, CHUNK), CHUNK)
+        return recv_f[where, :].astype(jnp.float32)
+
+    def place(block, first, offset):
+        piece = (block * inner + first) // part
+        start = piece // 2 * part + offset
+        return pl.ds(pl.multiple_of(start, CHUNK), CHUNK), piece % 2
+
+    def load_half(ref, own, block, first, offset):
+        where, side = place(block, first, offset)
+        value = ref[where, :].astype(jnp.float32)
+        return value if side == own else swap(value)
+
+    def store_half(ref, own, block, first, offset, value):
+        where, side = place(block, first, offset)
+        value = (value if side == own else swap(value)).astype(jnp.bfloat16)
+        if side == 0:
+            ref[where, :] = value
+        else:
+            ref[where, LANES // 2 :] = value[:, LANES // 2 :]
+
+    def transform(source, target, own):
+        load = functools.partial(load_half, source, own)
+        spread_blocks(inner, part, load, y_full, y_real)
+        filtered(
+            inner, f_full, f_real, g_full, g_real, y_full, y_real, h_full, h_real, z_full, z_real
+        )
+        gather_blocks(inner, part, z_full, z_real, functools.partial(store_half, target, own))
 
     for load in loads[7:]:
         load.wait()
     arrive_f()
-    spread_blocks(inner, block_of(recv_f), y_full, y_real, (low_full, low_real))
+    spread_blocks(inner, part, load_filter, y_full, y_real, (low_full, low_real))
     filter_spectrum(f_full, f_real, y_full, y_real, low_full, low_real, h_full, h_real)
-    arrive_g()
-    spread_blocks(inner, block_of(recv_g), y_full, y_real)
-    filtered(inner, f_full, f_real, g_full, g_real, y_full, y_real, h_full, h_real)
-    gather_blocks(inner, h_full, h_real, store)
-    start_y()
-    recv_y[at(me), :] = send_y[at(me), :]
-
-    mixed_copy = pltpu.make_async_copy(mixed_ref, mixed_hbm, out_sem.at[0])
-    normed_copy = pltpu.make_async_copy(normed_ref, normed_hbm, out_sem.at[1])
+    arrive_a()
+    transform(recv_a, send_ya, 0)
+    start_ya()
+    recv_ya[packed_at(me), :] = send_ya[packed_at(me), :]
+    arrive_b()
+    transform(recv_b, send_yb, 1)
+    start_yb()
+    recv_yb[packed_at(me), :] = send_yb[packed_at(me), :]
 
     def mix(block):
-        conv = recv_y[at(block), :].astype(jnp.float32)
+        half_a = recv_ya[packed_at(block), :].astype(jnp.float32)
+        half_b = recv_yb[packed_at(block), :].astype(jnp.float32)
+        top = jnp.where(lower, half_a, swap(half_b))
+        bottom = jnp.where(lower, swap(half_a), half_b)
+        conv = jnp.concatenate([top, bottom])
         mixed = query[at(block), :] * (conv + skip_ref[:, lanes(block)] * gated[at(block), :])
         query[at(block), :] = mixed
         mixed_ref[:, lanes(block)] = mixed.astype(jnp.bfloat16)
@@ -508,7 +556,8 @@
 
     def mix_next(j, carry):
         block = partner(n - 2 - j)
-        come_y(block).wait_recv()
+        come_ya(block).wait_recv()
+        come_yb(block).wait_recv()
         return carry + mix(block)
 
     sums[...] = lax.fori_loop(0, n - 1, mix_next, mix(me))
@@ -521,10 +570,8 @@
         device_id_type=MESH,
     )
     sum_copy.start()
-    mixed_copy.start()
-    leave_f()
-    leave_g()
-    leave_y()
+    for leave in (leave_f, leave_a, leave_b, leave_ya, leave_yb):
+        leave()
     sum_copy.wait()
     total = jnp.sum(sums[...] + other_sums[...], axis=1, keepdims=True)
     scale = lax.rsqrt(total / D + 1e-05)
@@ -535,9 +582,6 @@
         return carry
 
     lax.fori_loop(0, n, norm, 0)
-    normed_copy.start()
-    mixed_copy.wait()
-    normed_copy.wait()
 
 
 def channel_shards(q_proj, k_proj, v_proj, feat_filter, long_filter, skip_bias, norm_gain):
@@ -548,33 +592,34 @@
     tables = [jnp.asarray(t) for t in dft_tables(seq)]
     narrow, wide = jnp.bfloat16, jnp.float32
     scratch = [pltpu.VMEM(feat_filter.shape, wide), pltpu.VMEM((1, channels), wide)]
-    scratch += [pltpu.VMEM((1, channels), wide)] + [pltpu.VMEM((rows, channels), narrow)] * 2
+    scratch += [pltpu.VMEM((1, channels), wide)]
     scratch += [pltpu.VMEM((rows, channels), narrow)] * 3 + [pltpu.VMEM((rows, channels), wide)]
     scratch += [pltpu.VMEM(t.shape, narrow) for t in tables]
     scratch += [pltpu.VMEM((3, 16, channels), narrow)]
-    scratch += [pltpu.VMEM((seq, LANES), narrow)] * 6
+    scratch += [pltpu.VMEM((seq, LANES), narrow)] * 2
+    scratch += [pltpu.VMEM((seq // 2, LANES), narrow)] * 8
     scratch += [pltpu.VMEM((seq, LANES), wide)] * 2
     scratch += [pltpu.VMEM((rows, LANES), wide)] * 2
     scratch += spectrum_scratch(inner)
     scratch += [pltpu.SemaphoreType.DMA((11,))]
     scratch += [pltpu.SemaphoreType.DMA((3,))] * 2
-    scratch += [pltpu.SemaphoreType.DMA((n,))] * 6
-    scratch += [pltpu.SemaphoreType.DMA((2,))] * 2
-    away = pl.BlockSpec(memory_space=pl.ANY)
+    scratch += [pltpu.SemaphoreType.DMA((n,))] * 10
+    scratch += [pltpu.SemaphoreType.DMA((2,))]
+    away = pl.BlockSpec(memory_space=pltpu.HBM)
+    whole = pl.BlockSpec(memory_space=pltpu.VMEM)
     out = jax.ShapeDtypeStruct((rows, channels), narrow)
+    operands = [q_proj, k_proj, v_proj, long_filter, *tables, feat_filter]
+    operands += [skip_bias.reshape(1, -1), norm_gain.reshape(1, -1)]
     return tuple(pl.pallas_call(
         functools.partial(mixer_kernel, n, inner),
         out_shape=(out, out),
         in_specs=[away] * 11,
-        out_specs=(away, away),
+        out_specs=(whole, whole),
         scratch_shapes=scratch,
         compiler_params=pltpu.CompilerParams(
             collective_id=0, has_side_effects=True, vmem_limit_bytes=VMEM_BYTES
         ),
-    )(
-        q_proj, k_proj, v_proj, long_filter, *tables,
-        feat_filter, skip_bias.reshape(1, -1), norm_gain.reshape(1, -1),
-    ))
+    )(*[pltpu.with_memory_space_constraint(a, pltpu.HBM) for a in operands]))
 
 
 def solution(mesh):
@@ -582,8 +627,8 @@
         rows, channels = arrays[0].shape
         n = mesh.shape["seq"]
         seq = rows * n
-        whole_lanes = channels == LANES * n and n % 4 == 0 and mesh.shape["ch"] == 2
-        if whole_lanes and rows % 16 == 0 and seq % (2 * HALF * CHUNK) == 0 and seq <= 2048:
+        whole_lanes = channels == LANES * n and n % 4 == 0 and rows % 64 == 0 and mesh.shape["ch"] == 2
+        if whole_lanes and seq % (2 * HALF * CHUNK) == 0 and seq <= 2048:
             return channel_shards(*arrays)
         return shards(*arrays)
 

time: 61.8 us -> 62.6 us (1.013)
  Pallas kernels: 57.2 us -> 60 us
  local copies, waits for them, and re-layouts: 3.76 us -> 1.59 us
    pallas_call x1, Pallas kernels: 57.2 us -> 60 us  [channel_shards(): pl.pallas_call(functools.partial(mixer_kernel, n, inner), out_shape=(out,...]
    unnamed x2, local copies, waits for them, and re-layouts: 3.76 us -> 1.59 us
where the time goes in v5:
time: 62.6 us; the launch traced here: 62.2 us
  Pallas kernels  60 us (96%)
  local copies, waits for them, and re-layouts  1.59 us (3%)
  between operations  0.64 us (1%)
    pallas_call x1, Pallas kernels, channel_shards(): pl.pallas_call(functools.partial(mixer_kernel, n, inner), out_shape=(out,...  60 us
    unnamed x2, local copies, waits for them, and re-layouts  1.59 us

profile of v5, /device:TPU:0, one launch (start us, length us, event | category | flops | bytes accessed | tf_op | source)
XLA Modules:
  0.0 62.2 jit_solution(1558826209749334728)
XLA Ops:
  0.6 60.0 %shard_map.122 = (bf16[128,2048]{1,0:T(8,128)(2,1)S(1)}, bf16[128,2048]{1,0:T(8,128)(2,1)S(1)}) custom-call(bf16[128,2048]{1,0:T(8,128)(2,1)} %q_hbm.1, bf16[128,2048]{1,0:T(8,128)(2,1)} %k_hbm.1, bf16[128,2048]{1,0:T(8,128)(2,1)} %v_hbm.1, f32[128,2048]{1,0:T(8,128)} %filter_hbm.1, bf16[7,512,1024]{2,1,0:T(8,128)(2,1)} %constant.8.clone.f_full_hbm, ...), custom_call_target="tpu_custom_call" | custom-call | tf_op jit(solution)/shard_map/pallas_call | solution.py:613
  60.6 0.8 %copy.15 = bf16[128,2048]{1,0:T(8,128)(2,1)} copy(bf16[128,2048]{1,0:T(8,128)(2,1)S(1)} %get-tuple-element.4) | data formatting | bytes 1048576
  61.4 0.8 %copy.16 = bf16[128,2048]{1,0:T(8,128)(2,1)} copy(bf16[128,2048]{1,0:T(8,128)(2,1)S(1)} %get-tuple-element.5) | data formatting | bytes 1048576

commit v6 on v4

--- a/solution.py
+++ b/solution.py
@@ -13,7 +13,7 @@
 RADIX = 16
 HALF = RADIX // 2
 LANES = 128
-VMEM_BYTES = 62 * 2**20
+VMEM_BYTES = 48 * 2**20
 MESH = pl.DeviceIdType.MESH
 
 
@@ -178,13 +178,14 @@
         z = jnp.concatenate([pr, pi]).astype(jnp.bfloat16)
         h_real[i] = dot(g_real[i], z)
 
-    def step(k, carry):
-        pr, pi = product(dot(f_full[k, :, : 2 * inner], y_full[k]), h_full[k], inner)
+    ahead = dot(f_full[0, :, : 2 * inner], y_full[0])
+    for k in range(HALF - 1):
+        spectrum = ahead
+        if k + 1 < HALF - 1:
+            ahead = dot(f_full[k + 1, :, : 2 * inner], y_full[k + 1])
+        pr, pi = product(spectrum, h_full[k], inner)
         z = (jnp.concatenate([pr, pi]) * (2.0 / length)).astype(jnp.bfloat16)
         h_full[k] = dot(g_full[k], z)
-        return carry
-
-    lax.fori_loop(0, HALF - 1, step, 0)
 
 
 def gather_blocks(inner, h_full, h_real, store):
@@ -323,11 +324,11 @@
     n, inner,
     q_hbm, k_hbm, v_hbm, filter_hbm, f_full_hbm, f_real_hbm, g_full_hbm, g_real_hbm,
     feat_hbm, skip_hbm, gain_hbm,
-    mixed_hbm, normed_hbm,
-    feat_ref, skip_ref, gain_ref, mixed_ref, normed_ref, q_ref, k_ref, v_ref, filter_ref, f_full, f_real, g_full, g_real,
+    mixed_ref, normed_ref,
+    feat_ref, skip_ref, gain_ref, q_ref, k_ref, v_ref, filter_ref, f_full, f_real, g_full, g_real,
     tails, send_f, send_g, send_y, recv_f, recv_g, recv_y, query, gated, sums, other_sums,
     y_full, y_real, low_full, low_real, h_full, h_real,
-    local_sem, tail_send, tail_recv, f_send, f_recv, g_send, g_recv, y_send, y_recv, sum_sem, out_sem,
+    local_sem, tail_send, tail_recv, f_send, f_recv, g_send, g_recv, y_send, y_recv, sum_sem,
 ):
     me = lax.axis_index("seq")
     core = lax.axis_index("ch")
@@ -342,8 +343,7 @@
         return pl.ds(pl.multiple_of(block * LANES, LANES), LANES)
 
     def partner(j):
-        quarter = n // 4
-        offset = (3 - j % 4) * quarter + quarter - 1 - j // 4
+        offset = n // 2 + ((j + 1) // 2) * (2 * (j % 2) - 1)
         return lax.rem(me + offset, n)
 
     loads = [
@@ -496,9 +496,6 @@
     start_y()
     recv_y[at(me), :] = send_y[at(me), :]
 
-    mixed_copy = pltpu.make_async_copy(mixed_ref, mixed_hbm, out_sem.at[0])
-    normed_copy = pltpu.make_async_copy(normed_ref, normed_hbm, out_sem.at[1])
-
     def mix(block):
         conv = recv_y[at(block), :].astype(jnp.float32)
         mixed = query[at(block), :] * (conv + skip_ref[:, lanes(block)] * gated[at(block), :])
@@ -521,7 +518,6 @@
         device_id_type=MESH,
     )
     sum_copy.start()
-    mixed_copy.start()
     leave_f()
     leave_g()
     leave_y()
@@ -535,9 +531,6 @@
         return carry
 
     lax.fori_loop(0, n, norm, 0)
-    normed_copy.start()
-    mixed_copy.wait()
-    normed_copy.wait()
 
 
 def channel_shards(q_proj, k_proj, v_proj, feat_filter, long_filter, skip_bias, norm_gain):
@@ -548,7 +541,7 @@
     tables = [jnp.asarray(t) for t in dft_tables(seq)]
     narrow, wide = jnp.bfloat16, jnp.float32
     scratch = [pltpu.VMEM(feat_filter.shape, wide), pltpu.VMEM((1, channels), wide)]
-    scratch += [pltpu.VMEM((1, channels), wide)] + [pltpu.VMEM((rows, channels), narrow)] * 2
+    scratch += [pltpu.VMEM((1, channels), wide)]
     scratch += [pltpu.VMEM((rows, channels), narrow)] * 3 + [pltpu.VMEM((rows, channels), wide)]
     scratch += [pltpu.VMEM(t.shape, narrow) for t in tables]
     scratch += [pltpu.VMEM((3, 16, channels), narrow)]
@@ -559,22 +552,22 @@
     scratch += [pltpu.SemaphoreType.DMA((11,))]
     scratch += [pltpu.SemaphoreType.DMA((3,))] * 2
     scratch += [pltpu.SemaphoreType.DMA((n,))] * 6
-    scratch += [pltpu.SemaphoreType.DMA((2,))] * 2
-    away = pl.BlockSpec(memory_space=pl.ANY)
+    scratch += [pltpu.SemaphoreType.DMA((2,))]
+    away = pl.BlockSpec(memory_space=pltpu.HBM)
+    whole = pl.BlockSpec(memory_space=pltpu.VMEM)
     out = jax.ShapeDtypeStruct((rows, channels), narrow)
+    operands = [q_proj, k_proj, v_proj, long_filter, *tables, feat_filter]
+    operands += [skip_bias.reshape(1, -1), norm_gain.reshape(1, -1)]
     return tuple(pl.pallas_call(
         functools.partial(mixer_kernel, n, inner),
         out_shape=(out, out),
         in_specs=[away] * 11,
-        out_specs=(away, away),
+        out_specs=(whole, whole),
         scratch_shapes=scratch,
         compiler_params=pltpu.CompilerParams(
             collective_id=0, has_side_effects=True, vmem_limit_bytes=VMEM_BYTES
         ),
-    )(
-        q_proj, k_proj, v_proj, long_filter, *tables,
-        feat_filter, skip_bias.reshape(1, -1), norm_gain.reshape(1, -1),
-    ))
+    )(*[pltpu.with_memory_space_constraint(a, pltpu.HBM) for a in operands]))
 
 
 def solution(mesh):
@@ -582,8 +575,8 @@
         rows, channels = arrays[0].shape
         n = mesh.shape["seq"]
         seq = rows * n
-        whole_lanes = channels == LANES * n and n % 4 == 0 and mesh.shape["ch"] == 2
-        if whole_lanes and rows % 16 == 0 and seq % (2 * HALF * CHUNK) == 0 and seq <= 2048:
+        whole_lanes = channels == LANES * n and n % 4 == 0 and rows % 64 == 0 and mesh.shape["ch"] == 2
+        if whole_lanes and seq % (2 * HALF * CHUNK) == 0 and seq <= 2048:
             return channel_shards(*arrays)
         return shards(*arrays)
 

time: 61.8 us -> 52.6 us (0.85)
  Pallas kernels: 57.2 us -> 50.1 us
  local copies, waits for them, and re-layouts: 3.76 us -> 1.59 us
    pallas_call x1, Pallas kernels: 57.2 us -> 50.1 us  [channel_shards(): pl.pallas_call(functools.partial(mixer_kernel, n, inner), out_shape=(out,...]
    unnamed x2, local copies, waits for them, and re-layouts: 3.76 us -> 1.59 us
where the time goes in v6:
time: 52.6 us; the launch traced here: 52.4 us
  Pallas kernels  50.1 us (95%)
  local copies, waits for them, and re-layouts  1.59 us (3%)
  between operations  0.64 us (1%)
    pallas_call x1, Pallas kernels, channel_shards(): pl.pallas_call(functools.partial(mixer_kernel, n, inner), out_shape=(out,...  50.1 us
    unnamed x2, local copies, waits for them, and re-layouts  1.59 us

profile of v6, /device:TPU:0, one launch (start us, length us, event | category | flops | bytes accessed | tf_op | source)
XLA Modules:
  0.0 52.4 jit_solution(8623291997216873760)
XLA Ops:
  0.6 50.1 %shard_map.122 = (bf16[128,2048]{1,0:T(8,128)(2,1)S(1)}, bf16[128,2048]{1,0:T(8,128)(2,1)S(1)}) custom-call(bf16[128,2048]{1,0:T(8,128)(2,1)} %q_hbm.1, bf16[128,2048]{1,0:T(8,128)(2,1)} %k_hbm.1, bf16[128,2048]{1,0:T(8,128)(2,1)} %v_hbm.1, f32[128,2048]{1,0:T(8,128)} %filter_hbm.1, bf16[7,512,1024]{2,1,0:T(8,128)(2,1)} %constant.8.clone.f_full_hbm, ...), custom_call_target="tpu_custom_call" | custom-call | tf_op jit(solution)/shard_map/pallas_call | solution.py:561
  50.8 0.8 %copy.15 = bf16[128,2048]{1,0:T(8,128)(2,1)} copy(bf16[128,2048]{1,0:T(8,128)(2,1)S(1)} %get-tuple-element.4) | data formatting | bytes 1048576
  51.6 0.8 %copy.16 = bf16[128,2048]{1,0:T(8,128)(2,1)} copy(bf16[128,2048]{1,0:T(8,128)(2,1)S(1)} %get-tuple-element.5) | data formatting | bytes 1048576
